TPU v7x, 768 devices: a whole 4x8x12 slice. The times are simulated.
768 devices in a mesh: comp: 8 (over x, core), tile: 96 (over y, z).
Axes of the slice: x: 4, y: 8, z: 12, core: 2. Of those that a mesh axis runs over, the one named last changes fastest.
Arguments:
- initial: float32 [8, 12, 192, 384], P('comp', None, 'tile'), may hold values from -6 to 6
- cotangent: float32 [8, 12, 192, 384], P('comp', None, 'tile'), may hold values from -6 to 6
- spread_coef: float32 [8, 12, 192, 384], P('comp', None, 'tile'), may hold values from 0.4 to 1
- trajectory: float32 [4, 8, 12, 192, 384], P(None, 'comp', None, 'tile'), may hold values from 0.5 to 1.6
- mixing: float32 [8, 12, 12], P('comp')
- sea_mask: int32 [8, 192, 384], P('comp', 'tile'), may hold values 0 or 1
- src_group: int32 [8, 96, 96, 64], P('comp', 'tile'), may hold values from 0 to 7, as said below
- src_cell: int32 [8, 96, 96, 64], P('comp', 'tile'), may hold values from 0 to 767
- weight: float32 [8, 96, 96, 64], P('comp', 'tile'), may hold values from 0.25 to 1
- counts: int32 [8, 96, 96], P('comp', 'tile'), may hold values from 0 to 64, as said below
- dst_cell: int32 [8, 96, 96, 64], P('comp', 'tile'), may hold values from 0 to 767
Outputs:
- final_state: float32 [8, 12, 192, 384], P('comp', None, 'tile')
- gradient: float32 [8, 12, 192, 384], P('comp', None, 'tile')
Inputs may be any that keep to these rules, and one draw needn't show every extreme that they name: `src_group`: the source group of a slot is an ocean group (index 6 or more) when the receiving group is an atmosphere group (index under 6), and an atmosphere group otherwise; it is the same for all slots of one pair of tiles. `counts`: in every group one receiving tile gets all 64 slots live from every sending tile.
All inputs are finite; a program needn't handle non-finite values. No bound on the sum of `sea_mask` on one device may be relied on, other than what follows from the above.
Results may differ from a plain program's by a relative error of at most 0.00015.
Values sent between devices are 32-bit elements; how exact they have to be, the bound alone decides.
A program may use at most 32 MiB of HBM per device.

v0:
```python
import jax
import jax.numpy as jnp
from jax import lax
from jax.sharding import PartitionSpec as P

INTERVALS = 2
SUBSTEPS = 2


SPREAD = 0.12


def with_halo(block, sides, width):
    for axis, dim in sides:
        count = lax.axis_size(axis)
        forward = [(i, i + 1) for i in range(count - 1)]
        backward = [(target, source) for source, target in forward]
        low = lax.ppermute(
            lax.slice_in_dim(block, block.shape[dim] - width, None, axis=dim), axis, forward
        )
        high = lax.ppermute(lax.slice_in_dim(block, 0, width, axis=dim), axis, backward)
        block = jnp.concatenate([low, block, high], axis=dim)
    return block


def laplace_valid(padded):
    wide = jnp.pad(padded, ((0, 0), (0, 0), (0, 0), (1, 1)))
    total = padded[:, :, 2:, :] + padded[:, :, :-2, :]
    total = total + wide[:, :, 1:-1, 2:] + wide[:, :, 1:-1, :-2]
    return total - 4.0 * padded[:, :, 1:-1, :]


def vertical(matrix, field_state):
    level_count = field_state.shape[1]
    flat_field = field_state.reshape(level_count, -1)
    product = jnp.dot(
        matrix, flat_field, precision=lax.Precision.HIGHEST, preferred_element_type=jnp.float32
    )
    return product.reshape(field_state.shape)


def shallow_rims(values):
    return with_halo(values, (("tile", 2),), 1)


def forward_shallow(field_state, spread_coef, matrix, factor):
    padded = shallow_rims(spread_coef * field_state)
    diffused = field_state + SPREAD * spread_coef * laplace_valid(padded)
    return factor * vertical(matrix, diffused)


def adjoint_shallow(field_state, spread_coef, matrix, factor):
    mixed_back = vertical(jnp.transpose(matrix), factor * field_state)
    padded = shallow_rims(spread_coef * mixed_back)
    return mixed_back + SPREAD * spread_coef * laplace_valid(padded)


def slot_exchange(values):
    return lax.all_to_all(values, "tile", split_axis=0, concat_axis=0, tiled=True)


def couple_forward(field_state, sea_cells, gather_index, send_weight, dst_flat):
    cell_count = sea_cells.shape[0]
    surface = field_state[0, 0].reshape(1, cell_count)
    everyone = lax.all_gather(surface, "comp", axis=0, tiled=True).reshape(-1)
    values = send_weight * everyone[gather_index]
    received = slot_exchange(values)
    forcing = (
        jax.ops.segment_sum(received.reshape(-1), dst_flat, num_segments=cell_count) * sea_cells
    )
    return field_state.at[0, 0].add(forcing.reshape(field_state.shape[2], field_state.shape[3]))


def couple_adjoint(field_state, sea_cells, gather_index, send_weight, dst_flat, group_count):
    cell_count = sea_cells.shape[0]
    masked = field_state[0, 0].reshape(-1) * sea_cells
    pulled = masked[dst_flat].reshape(send_weight.shape)
    returned = slot_exchange(pulled)
    terms = jax.ops.segment_sum(
        (returned * send_weight).reshape(-1),
        gather_index.reshape(-1),
        num_segments=group_count * cell_count,
    )
    own_part = lax.psum_scatter(
        terms.reshape(group_count, cell_count), "comp", scatter_dimension=0, tiled=True
    )
    return field_state.at[0, 0].add(own_part.reshape(field_state.shape[2], field_state.shape[3]))


def per_device(
    initial,
    cotangent,
    spread_coef,
    trajectory,
    mixing,
    sea_mask,
    src_group,
    src_cell,
    weight,
    counts,
    dst_cell,
):
    group_count = lax.axis_size("comp")
    cell_count = initial.shape[2] * initial.shape[3]
    slot_count = weight.shape[3]
    matrix = mixing[0]
    sea_cells = sea_mask[0].reshape(-1).astype(jnp.float32)
    live_mask = jnp.arange(slot_count, dtype=jnp.int32)[None, :] < counts[0, 0][:, None]
    send_weight = weight[0, 0] * live_mask.astype(jnp.float32)
    gather_index = src_group[0, 0] * cell_count + src_cell[0, 0]
    dst_flat = dst_cell[0, 0].reshape(-1)
    factors = trajectory[:, 0]
    forward_now = initial
    for interval in range(INTERVALS):
        forward_now = couple_forward(forward_now, sea_cells, gather_index, send_weight, dst_flat)
        for substep in range(SUBSTEPS):
            step_index = interval * SUBSTEPS + substep
            forward_now = forward_shallow(
                forward_now, spread_coef, matrix, factors[step_index : step_index + 1]
            )
    adjoint_now = cotangent
    for interval in reversed(range(INTERVALS)):
        for back_step in range(SUBSTEPS):
            step_index = interval * SUBSTEPS + SUBSTEPS - 1 - back_step
            adjoint_now = adjoint_shallow(
                adjoint_now, spread_coef, matrix, factors[step_index : step_index + 1]
            )
        adjoint_now = couple_adjoint(
            adjoint_now, sea_cells, gather_index, send_weight, dst_flat, group_count
        )
    return (forward_now, adjoint_now)


def solution(mesh):
    return jax.shard_map(
        per_device,
        mesh=mesh,
        in_specs=(
            P("comp", None, "tile", None),
            P("comp", None, "tile", None),
            P("comp", None, "tile", None),
            P(None, "comp", None, "tile", None),
            P("comp", None, None),
            P("comp", "tile", None),
            P("comp", "tile", None, None),
            P("comp", "tile", None, None),
            P("comp", "tile", None, None),
            P("comp", "tile", None),
            P("comp", "tile", None, None),
        ),
        out_specs=(P("comp", None, "tile", None), P("comp", None, "tile", None)),
        check_vma=False,
    )
```

profile of v0, /device:TPU:1, one launch (start us, length us, event | category | flops | bytes accessed | tf_op | source)
XLA Modules:
  0.0 536.7 jit_solution(4675438206124194760)
XLA Ops:
  0.6 0.8 copy.75
  1.4 23.0 %all-gather = f32[8,1,768]{2,1,0:T(1,128)S(1)} all-gather(f32[1,1,768]{2,1,0:T(1,128)S(1)} %reshape.607), channel_id=1, replica_groups=mesh['comp'=8,'tile'=96] {'comp'}, dimensions={0}, use_global_device_ids=true | all-gather | bytes 27648 | tf_op jit(solution)/shard_map/all_gather | solution.py:65
  25.4 34.3 %gather_fusion = f32[6144]{0:T(1024)S(1)} fusion(f32[6144]{0:T(1024)S(1)} %bitcast.146, s32[6144]{0:T(1024)S(1)} %broadcast_clamp_fusion.1), kind=kCustom, calls=%fused_computation | custom fusion | bytes 73728 | tf_op jit(solution)/shard_map/gather | solution.py:66
  60.5 13.2 %all-to-all-start = ((f32[96,1,64]{2,1,0:T(1,128)}), f32[96,1,64]{2,1,0:T(1,128)S(1)}, u32[]{:S(2)}, u32[]{:S(2)}) async-start(f32[96,1,64]{2,1,0:T(1,128)} %bitcast.8), calls=%async_computation | async-start | bytes 98304 | tf_op jit(solution)/shard_map/all_to_all | solution.py:59
  73.8 0.7 copy-done.6
  75.7 11.0 %all-to-all-done = f32[96,1,64]{2,1,0:T(1,128)S(1)} async-done(((f32[96,1,64]{2,1,0:T(1,128)}), f32[96,1,64]{2,1,0:T(1,128)S(1)}, u32[]{:S(2)}, u32[]{:S(2)}) %all-to-all-start) | async-done | bytes 24608 | tf_op jit(solution)/shard_map/all_to_all | solution.py:59
  87.2 0.8 reduce.24
  88.1 42.9 %scatter_custom_fusion = f32[768]{0:T(1024)S(1)} fusion(s32[6144]{0:T(1024)S(1)} %reshape.569, f32[6144]{0:T(1024)S(1)} %reshape.571, f32[]{:T(128)} %constant.104.clone.1), kind=kCustom, calls=%fused_computation.157 | custom fusion | flops 6144 | bytes 3076 | tf_op jit(solution)/shard_map/scatter-add | solution.py:69
  131.1 2.3 collective-permute-start.1
  133.4 1.3 collective-permute-start
  134.7 4.0 collective-permute-start.9
  138.7 1.3 collective-permute-start.8
  140.7 2.5 collective-permute-done.8
  144.0 1.9 collective-permute-start.11
  145.9 1.3 collective-permute-start.10
  147.6 1.3 dynamic-slice.28
  148.9 1.5 collective-permute-done.10
  150.8 24.8 %gather_fusion.2 = f32[6144]{0:T(1024)S(1)} fusion(f32[768]{0:T(1024)S(1)} %mul.239, s32[6144]{0:T(1024)S(1)} %broadcast_clamp_fusion), kind=kCustom, calls=%fused_computation.2 | custom fusion | bytes 73728 | tf_op jit(solution)/shard_map/gather | solution.py:77
  176.3 15.7 %all-to-all-start.2 = ((f32[96,1,64]{2,1,0:T(1,128)}), f32[96,1,64]{2,1,0:T(1,128)S(1)}, u32[]{:S(2)}, u32[]{:S(2)}) async-start(f32[96,1,64]{2,1,0:T(1,128)} %bitcast.18), calls=%async_computation.2 | async-start | bytes 98304 | tf_op jit(solution)/shard_map/all_to_all | solution.py:59
  192.0 2.7 collective-permute-start.3
  194.7 1.3 collective-permute-start.2
  196.0 9.0 %all-to-all-done.2 = f32[96,1,64]{2,1,0:T(1,128)S(1)} async-done(((f32[96,1,64]{2,1,0:T(1,128)}), f32[96,1,64]{2,1,0:T(1,128)S(1)}, u32[]{:S(2)}, u32[]{:S(2)}) %all-to-all-start.2) | async-done | bytes 24608 | tf_op jit(solution)/shard_map/all_to_all | solution.py:59
  205.1 0.8 reduce.26
  205.9 38.5 %scatter_custom_fusion.2 = f32[6144]{0:T(1024)S(1)} fusion(s32[6144]{0:T(1024)S(1)} %reshape.585, f32[6144]{0:T(1024)S(1)} %fusion.50, f32[]{:T(128)} %constant.104.clone.1), kind=kCustom, calls=%fused_computation.128 | custom fusion | flops 6144 | bytes 24580 | tf_op jit(solution)/shard_map/scatter-add | solution.py:79
  244.5 27.8 %all-reduce.8 = f32[8,768]{1,0:T(8,128)S(1)} all-reduce(f32[8,768]{1,0:T(8,128)S(1)} %reshape.527), channel_id=2, replica_groups=mesh['comp'=8,'tile'=96] {'comp'}, use_global_device_ids=true, to_apply=%region_3.4.clone | all-reduce | flops 6144 | bytes 49152
  273.4 2.3 collective-permute-start.13
  275.7 1.3 collective-permute-start.12
  277.3 2.9 collective-permute-done.12
  281.1 17.6 %all-gather.1 = f32[8,1,768]{2,1,0:T(1,128)S(1)} all-gather(f32[1,1,768]{2,1,0:T(1,128)S(1)} %reshape.609), channel_id=1, replica_groups=mesh['comp'=8,'tile'=96] {'comp'}, dimensions={0}, use_global_device_ids=true | all-gather | bytes 27648 | tf_op jit(solution)/shard_map/all_gather | solution.py:65
  298.8 34.3 %gather_fusion.1 = f32[6144]{0:T(1024)S(1)} fusion(f32[6144]{0:T(1024)S(1)} %bitcast.147, s32[6144]{0:T(1024)S(1)} %broadcast_clamp_fusion.1), kind=kCustom, calls=%fused_computation.1 | custom fusion | bytes 73728 | tf_op jit(solution)/shard_map/gather | solution.py:66
  333.1 0.7 fusion.1
  333.8 10.3 %all-to-all-start.1 = ((f32[96,1,64]{2,1,0:T(1,128)}), f32[96,1,64]{2,1,0:T(1,128)S(1)}, u32[]{:S(2)}, u32[]{:S(2)}) async-start(f32[96,1,64]{2,1,0:T(1,128)} %bitcast.12), calls=%async_computation.1 | async-start | bytes 98304 | tf_op jit(solution)/shard_map/all_to_all | solution.py:59
  344.4 12.8 %all-to-all-done.1 = f32[96,1,64]{2,1,0:T(1,128)S(1)} async-done(((f32[96,1,64]{2,1,0:T(1,128)}), f32[96,1,64]{2,1,0:T(1,128)S(1)}, u32[]{:S(2)}, u32[]{:S(2)}) %all-to-all-start.1) | async-done | bytes 24608 | tf_op jit(solution)/shard_map/all_to_all | solution.py:59
  357.2 0.8 reduce.25
  358.0 42.9 %scatter_custom_fusion.1 = f32[768]{0:T(1024)S(1)} fusion(s32[6144]{0:T(1024)S(1)} %reshape.569, f32[6144]{0:T(1024)S(1)} %reshape.579, f32[]{:T(128)} %constant.104.clone.1), kind=kCustom, calls=%fused_computation.155 | custom fusion | flops 6144 | bytes 3076 | tf_op jit(solution)/shard_map/scatter-add | solution.py:69
  401.0 2.3 collective-permute-start.5
  403.3 1.3 collective-permute-start.4
  404.6 4.0 collective-permute-start.15
  408.6 1.3 collective-permute-start.14
  410.2 2.9 collective-permute-done.14
  414.0 1.9 collective-permute-start.7
  415.9 1.3 collective-permute-start.6
  417.2 24.8 %gather_fusion.3 = f32[6144]{0:T(1024)S(1)} fusion(f32[768]{0:T(1024)S(1)} %mul.251, s32[6144]{0:T(1024)S(1)} %broadcast_clamp_fusion), kind=kCustom, calls=%fused_computation.3 | custom fusion | bytes 73728 | tf_op jit(solution)/shard_map/gather | solution.py:77
  442.7 15.3 %all-to-all-start.3 = ((f32[96,1,64]{2,1,0:T(1,128)}), f32[96,1,64]{2,1,0:T(1,128)S(1)}, u32[]{:S(2)}, u32[]{:S(2)}) async-start(f32[96,1,64]{2,1,0:T(1,128)} %bitcast.21), calls=%async_computation.3 | async-start | bytes 98304 | tf_op jit(solution)/shard_map/all_to_all | solution.py:59
  459.4 11.7 %all-to-all-done.3 = f32[96,1,64]{2,1,0:T(1,128)S(1)} async-done(((f32[96,1,64]{2,1,0:T(1,128)}), f32[96,1,64]{2,1,0:T(1,128)S(1)}, u32[]{:S(2)}, u32[]{:S(2)}) %all-to-all-start.3) | async-done | bytes 24608 | tf_op jit(solution)/shard_map/all_to_all | solution.py:59
  471.1 0.8 reduce.27
  472.0 38.5 %scatter_custom_fusion.3 = f32[6144]{0:T(1024)S(1)} fusion(s32[6144]{0:T(1024)S(1)} %reshape.585, f32[6144]{0:T(1024)S(1)} %fusion.49, f32[]{:T(128)} %constant.104.clone.1), kind=kCustom, calls=%fused_computation.126 | custom fusion | flops 6144 | bytes 24580 | tf_op jit(solution)/shard_map/scatter-add | solution.py:79
  510.5 24.9 %all-reduce.9 = f32[8,768]{1,0:T(8,128)S(1)} all-reduce(f32[8,768]{1,0:T(8,128)S(1)} %reshape.533), channel_id=3, replica_groups=mesh['comp'=8,'tile'=96] {'comp'}, use_global_device_ids=true, to_apply=%region_5.6.clone | all-reduce | flops 6144 | bytes 49152
  (149 shorter events, 13.5 us)
Async XLA Ops:
  1.4 23.0 %copy-start.5 = (f32[1,1,96,64]{2,3,1,0:T(8,128)S(1)}, f32[1,1,96,64]{2,3,1,0:T(8,128)}, u32[]{:S(2)}) copy-start(f32[1,1,96,64]{2,3,1,0:T(8,128)} %param.27) | copy-start | bytes 73732
  24.4 0.8 copy-start.7
  24.4 0.8 copy-start.8
  25.4 34.4 %copy-start.9 = (s32[1,1,96]{2,1,0:T(1,128)S(1)}, s32[1,1,96]{2,1,0:T(1,128)}, u32[]{:S(2)}) copy-start(s32[1,1,96]{2,1,0:T(1,128)} %param.28) | copy-start | bytes 1156
  59.7 14.0 %copy-start.1 = (f32[4,1,12,2,384]{4,3,2,1,0:T(2,128)S(1)}, f32[4,1,12,2,384]{4,3,2,1,0:T(2,128)}, u32[]{:S(2)}) copy-start(f32[4,1,12,2,384]{4,3,2,1,0:T(2,128)} %param.22) | copy-start | bytes 442372
  60.5 13.2 %copy-start.4 = (f32[1,12,2,384]{3,2,1,0:T(2,128)S(1)}, f32[1,12,2,384]{3,2,1,0:T(2,128)}, u32[]{:S(2)}) copy-start(f32[1,12,2,384]{3,2,1,0:T(2,128)} %param.20) | copy-start | bytes 110596
  60.5 14.3 %copy-start.2 = (f32[1,12,12]{2,0,1:T(1,128)S(1)}, f32[1,12,12]{2,0,1:T(1,128)}, u32[]{:S(2)}) copy-start(f32[1,12,12]{2,0,1:T(1,128)} %param.23) | copy-start | bytes 1732
  60.5 26.2 %all-to-all-start = ((f32[96,1,64]{2,1,0:T(1,128)}), f32[96,1,64]{2,1,0:T(1,128)S(1)}, u32[]{:S(2)}, u32[]{:S(2)}) async-start(f32[96,1,64]{2,1,0:T(1,128)} %bitcast.8), calls=%async_computation | async-start | bytes 98304 | tf_op jit(solution)/shard_map/all_to_all | solution.py:59
  73.8 0.8 copy-start.6
  75.0 0.7 copy-start.10
  88.1 42.9 %copy-start = (f32[1,12,2,384]{3,2,1,0:T(2,128)S(1)}, f32[1,12,2,384]{3,2,1,0:T(2,128)}, u32[]{:S(2)}) copy-start(f32[1,12,2,384]{3,2,1,0:T(2,128)} %param.21) | copy-start | bytes 110596
  131.1 8.9 %collective-permute-start.1 = (f32[1,12,1,384]{3,2,1,0:T(1,128)S(1)}, f32[1,12,1,384]{3,2,1,0:T(1,128)S(1)}, u32[]{:S(2)}, u32[]{:S(2)}) collective-permute-start(f32[1,12,1,384]{3,2,1,0:T(1,128)S(1)} %get-tuple-element.76), channel_id=1, source_target_pairs={{0,1},{1,2},{2,3},{3,4},{4,5},{5,6},{6,7},{7,8},{8,9},{9,10},{10,1... | collective-permute-start | bytes 55304 | tf_op jit(solution)/shard_map/ppermute | solution.py:18
  133.4 6.6 %collective-permute-start = (f32[1,12,1,384]{3,2,1,0:T(1,128)S(1)}, f32[1,12,1,384]{3,2,1,0:T(1,128)S(1)}, u32[]{:S(2)}, u32[]{:S(2)}) collective-permute-start(f32[1,12,1,384]{3,2,1,0:T(1,128)S(1)} %get-tuple-element.77), channel_id=1, source_target_pairs={{1,0},{2,1},{3,2},{4,3},{5,4},{6,5},{7,6},{8,7},{9,8},{10,9},{11,1... | collective-permute-start | bytes 55304 | tf_op jit(solution)/shard_map/ppermute | solution.py:21
  134.7 6.0 %collective-permute-start.9 = (f32[1,12,1,384]{3,2,1,0:T(1,128)S(1)}, f32[1,12,1,384]{3,2,1,0:T(1,128)S(1)}, u32[]{:S(2)}, u32[]{:S(2)}) collective-permute-start(f32[1,12,1,384]{3,2,1,0:T(1,128)S(1)} %get-tuple-element.66), channel_id=1, source_target_pairs={{0,1},{1,2},{2,3},{3,4},{4,5},{5,6},{6,7},{7,8},{8,9},{9,10},{10,1... | collective-permute-start | bytes 55304 | tf_op jit(solution)/shard_map/ppermute | solution.py:18
  138.7 4.5 collective-permute-start.8
  144.0 5.0 collective-permute-start.11
  145.9 4.5 collective-permute-start.10
  176.3 28.8 %all-to-all-start.2 = ((f32[96,1,64]{2,1,0:T(1,128)}), f32[96,1,64]{2,1,0:T(1,128)S(1)}, u32[]{:S(2)}, u32[]{:S(2)}) async-start(f32[96,1,64]{2,1,0:T(1,128)} %bitcast.18), calls=%async_computation.2 | async-start | bytes 98304 | tf_op jit(solution)/shard_map/all_to_all | solution.py:59
  192.0 85.0 %collective-permute-start.3 = (f32[1,12,1,384]{3,2,1,0:T(1,128)S(1)}, f32[1,12,1,384]{3,2,1,0:T(1,128)S(1)}, u32[]{:S(2)}, u32[]{:S(2)}) collective-permute-start(f32[1,12,1,384]{3,2,1,0:T(1,128)S(1)} %get-tuple-element.74), channel_id=1, source_target_pairs={{0,1},{1,2},{2,3},{3,4},{4,5},{5,6},{6,7},{7,8},{8,9},{9,10},{10,1... | collective-permute-start | bytes 55304 | tf_op jit(solution)/shard_map/ppermute | solution.py:18
  194.7 82.3 %collective-permute-start.2 = (f32[1,12,1,384]{3,2,1,0:T(1,128)S(1)}, f32[1,12,1,384]{3,2,1,0:T(1,128)S(1)}, u32[]{:S(2)}, u32[]{:S(2)}) collective-permute-start(f32[1,12,1,384]{3,2,1,0:T(1,128)S(1)} %get-tuple-element.75), channel_id=1, source_target_pairs={{1,0},{2,1},{3,2},{4,3},{5,4},{6,5},{7,6},{8,7},{9,8},{10,9},{11,1... | collective-permute-start | bytes 55304 | tf_op jit(solution)/shard_map/ppermute | solution.py:21
  273.4 3.9 collective-permute-start.13
  275.7 4.5 collective-permute-start.12
  333.8 23.3 %all-to-all-start.1 = ((f32[96,1,64]{2,1,0:T(1,128)}), f32[96,1,64]{2,1,0:T(1,128)S(1)}, u32[]{:S(2)}, u32[]{:S(2)}) async-start(f32[96,1,64]{2,1,0:T(1,128)} %bitcast.12), calls=%async_computation.1 | async-start | bytes 98304 | tf_op jit(solution)/shard_map/all_to_all | solution.py:59
  401.0 8.9 %collective-permute-start.5 = (f32[1,12,1,384]{3,2,1,0:T(1,128)S(1)}, f32[1,12,1,384]{3,2,1,0:T(1,128)S(1)}, u32[]{:S(2)}, u32[]{:S(2)}) collective-permute-start(f32[1,12,1,384]{3,2,1,0:T(1,128)S(1)} %get-tuple-element.72), channel_id=1, source_target_pairs={{0,1},{1,2},{2,3},{3,4},{4,5},{5,6},{6,7},{7,8},{8,9},{9,10},{10,1... | collective-permute-start | bytes 55304 | tf_op jit(solution)/shard_map/ppermute | solution.py:18
  403.3 6.6 %collective-permute-start.4 = (f32[1,12,1,384]{3,2,1,0:T(1,128)S(1)}, f32[1,12,1,384]{3,2,1,0:T(1,128)S(1)}, u32[]{:S(2)}, u32[]{:S(2)}) collective-permute-start(f32[1,12,1,384]{3,2,1,0:T(1,128)S(1)} %get-tuple-element.73), channel_id=1, source_target_pairs={{1,0},{2,1},{3,2},{4,3},{5,4},{6,5},{7,6},{8,7},{9,8},{10,9},{11,1... | collective-permute-start | bytes 55304 | tf_op jit(solution)/shard_map/ppermute | solution.py:21
  404.6 5.6 %collective-permute-start.15 = (f32[1,12,1,384]{3,2,1,0:T(1,128)S(1)}, f32[1,12,1,384]{3,2,1,0:T(1,128)S(1)}, u32[]{:S(2)}, u32[]{:S(2)}) collective-permute-start(f32[1,12,1,384]{3,2,1,0:T(1,128)S(1)} %get-tuple-element.58), channel_id=1, source_target_pairs={{0,1},{1,2},{2,3},{3,4},{4,5},{5,6},{6,7},{7,8},{8,9},{9,10},{10,1... | collective-permute-start | bytes 55304 | tf_op jit(solution)/shard_map/ppermute | solution.py:18
  408.6 4.5 collective-permute-start.14
  414.0 44.1 %collective-permute-start.7 = (f32[1,12,1,384]{3,2,1,0:T(1,128)S(1)}, f32[1,12,1,384]{3,2,1,0:T(1,128)S(1)}, u32[]{:S(2)}, u32[]{:S(2)}) collective-permute-start(f32[1,12,1,384]{3,2,1,0:T(1,128)S(1)} %get-tuple-element.70), channel_id=1, source_target_pairs={{0,1},{1,2},{2,3},{3,4},{4,5},{5,6},{6,7},{7,8},{8,9},{9,10},{10,1... | collective-permute-start | bytes 55304 | tf_op jit(solution)/shard_map/ppermute | solution.py:18
  415.9 42.2 %collective-permute-start.6 = (f32[1,12,1,384]{3,2,1,0:T(1,128)S(1)}, f32[1,12,1,384]{3,2,1,0:T(1,128)S(1)}, u32[]{:S(2)}, u32[]{:S(2)}) collective-permute-start(f32[1,12,1,384]{3,2,1,0:T(1,128)S(1)} %get-tuple-element.71), channel_id=1, source_target_pairs={{1,0},{2,1},{3,2},{4,3},{5,4},{6,5},{7,6},{8,7},{9,8},{10,9},{11,1... | collective-permute-start | bytes 55304 | tf_op jit(solution)/shard_map/ppermute | solution.py:21
  442.7 28.4 %all-to-all-start.3 = ((f32[96,1,64]{2,1,0:T(1,128)}), f32[96,1,64]{2,1,0:T(1,128)S(1)}, u32[]{:S(2)}, u32[]{:S(2)}) async-start(f32[96,1,64]{2,1,0:T(1,128)} %bitcast.21), calls=%async_computation.3 | async-start | bytes 98304 | tf_op jit(solution)/shard_map/all_to_all | solution.py:59
  536.1 0.6 copy-start.3
where the time goes:
time: 541 us; the launch traced here: 537 us
  other arithmetic  171 us (32%)
  local copies, waits for them, and re-layouts  128 us (24%)
  blocking collectives  93.4 us (17%)
  starting transfers between devices  86.2 us (16%)
  waiting for transfers between devices  54.4 us (10%)
    scatter-add x2, other arithmetic, couple_forward(): jax.ops.segment_sum(received.reshape(-1), dst_flat, num_segments=cell_count)  85.8 us
    scatter-add x2, other arithmetic, couple_adjoint(): jax.ops.segment_sum((returned * send_weight).reshape(-1), gather_index.re...  77 us
    gather x4, local copies, waits for them, and re-layouts, couple_forward(): values = send_weight * everyone[gather_index]  68.7 us
    all_to_all x4, starting transfers between devices, slot_exchange(): lax.all_to_all(values, 'tile', split_axis=0, concat_axis=0, tiled=True)  54.5 us
    unnamed x2, blocking collectives  52.7 us
    gather x2, local copies, waits for them, and re-layouts, couple_adjoint(): pulled = masked[dst_flat].reshape(send_weight.shape)  49.6 us
    all_to_all x4, waiting for transfers between devices, slot_exchange(): lax.all_to_all(values, 'tile', split_axis=0, concat_axis=0, tiled=True)  44.5 us
    all_gather x2, blocking collectives, couple_forward(): everyone = lax.all_gather(surface, 'comp', axis=0, tiled=True).reshape(-1)  40.6 us
  transfers between devices with their start and end apart: 20, of which 8 were waited for; matrix products, arithmetic and copies ran while one was open for 13% of the time, Pallas kernels for 0%

commit v1 on v0

v1 whole, which is shorter than its diff:
```python
import functools

import jax
import jax.numpy as jnp
from jax import lax
from jax.experimental import pallas as pl
from jax.experimental.pallas import tpu as pltpu
from jax.sharding import PartitionSpec as P

MESH = pl.DeviceIdType.MESH
SPREAD = 0.12
NG, NT, LEV, COLS, CAP = 8, 96, 12, 384, 64
HI = 6
F32, BF16, I32 = jnp.float32, jnp.bfloat16, jnp.int32

S0, SP, U1, T2, F1, T0, A1, U2, FF1, TB1, F2, Q1, S1, A2, FF2, TB2 = range(16)


def kernel(
    init_ref, cot_ref, spread_ref, traj_ref, mix_ref, sea_ref, srcg_ref, srcc_ref, w_ref, cnt_ref, dst_ref,
    outf_ref, outg_ref,
    sp, u1, t2, f1, t0, u2, f2, ff1, ff2, q1, ev1, ev2, ts1, ts2, tr1, tr2, snd1, snd2, rcv1, rcv2,
    wa, xa, ya, wb, own1, own3, adj, mb, mtb, seat, mtab, gi, slo, shi, wv, rlo, rrow, rw, val, onehot,
    ssem, rsem,
):
    g = lax.axis_index("comp")
    t = lax.axis_index("tile")
    right, left = lax.rem(t + 1, NT), lax.rem(t + NT - 1, NT)

    barrier = pltpu.get_barrier_semaphore()

    @pl.loop(1, NT)
    def _(j):
        pl.semaphore_signal(barrier, inc=1, device_id=(g, lax.rem(t + j, NT)), device_id_type=MESH)

    @pl.loop(1, NG)
    def _(j):
        pl.semaphore_signal(barrier, inc=1, device_id=(lax.rem(g + j, NG), t), device_id_type=MESH)

    def remote(k, src, dst, dev):
        return pltpu.make_async_remote_copy(
            src_ref=src, dst_ref=dst, send_sem=ssem.at[k], recv_sem=rsem.at[k], device_id=dev, device_id_type=MESH
        )

    def halo_send(k, buf):
        remote(k, buf.at[2:4], buf.at[0:2], (g, right)).start()
        remote(k, buf.at[2:4], buf.at[4:6], (g, left)).start()

    def wait_bytes(sem, k, ref):
        pltpu.make_async_copy(ref, ref, sem.at[k]).wait()

    def halo_recv(k, buf):
        wait_bytes(rsem, k, buf.at[0:4])

    def halo_sent(k, buf):
        wait_bytes(ssem, k, buf.at[0:4])

    def gather_send(k, ev):
        @pl.loop(1, NG)
        def _(j):
            remote(k, ev.at[g], ev.at[g], (lax.rem(g + j, NG), t)).start()

    def sum_send(k, ts, tr):
        @pl.loop(1, NG)
        def _(j):
            d = lax.rem(g + j, NG)
            remote(k, ts.at[d], tr.at[g], (d, t)).start()
        tr[g] = ts[g]

    def slots_send(k, snd, rcv):
        @pl.loop(1, NT)
        def _(j):
            d = lax.rem(t + j, NT)
            remote(k, snd.at[d], rcv.at[t], (g, d)).start()
        rcv[t] = snd[t]

    def strip(ref, r):
        return ref[:, r, :]

    lane = lax.broadcasted_iota(I32, (LEV, COLS), 1)

    def laplace(w, r):
        mid = w[r]
        west = jnp.where(lane == 0, 0.0, pltpu.roll(mid, 1, 1))
        east = jnp.where(lane == COLS - 1, 0.0, pltpu.roll(mid, COLS - 1, 1))
        return w[r + 1] + w[r - 1] + east + west - 4.0 * mid

    def mix_row(x, r, cols):
        parts = []
        for c in range(3):
            ls = slice(c * 128, (c + 1) * 128)
            acc = cols[0] * x[r, 0:1, ls]
            for m in range(1, LEV):
                acc = acc + cols[m] * x[r, m : m + 1, ls]
            parts.append(acc)
        return jnp.concatenate(parts, axis=1)

    def forward_pair(f, ta, tb_row, put):
        @pl.loop(0, 6)
        def _(r):
            wa[r] = sp[r] * f[r]

        @pl.loop(1, 5)
        def _(r):
            xa[r] = f[r] + SPREAD * sp[r] * laplace(wa, r)

        @pl.loop(1, 5)
        def _(r):
            y = ta[r] * mix_row(xa, r, mb)
            ya[r] = y
            wb[r] = sp[r] * y

        @pl.loop(2, 4)
        def _(r):
            xa[r] = ya[r] + SPREAD * sp[r] * laplace(wb, r)

        for r in (2, 3):
            put(r, tb_row(r) * mix_row(xa, r, mb))

    def adjoint_pair(u, ta):
        @pl.loop(0, 6)
        def _(r):
            wa[r] = sp[r] * u[r]

        @pl.loop(1, 5)
        def _(r):
            xa[r] = ta[r] * (u[r] + SPREAD * sp[r] * laplace(wa, r))

        @pl.loop(1, 5)
        def _(r):
            y = mix_row(xa, r, mtb)
            ya[r] = y
            wb[r] = sp[r] * y

        @pl.loop(2, 4)
        def _(r):
            adj[r] = ya[r] + SPREAD * sp[r] * laplace(wb, r)

    def surface_rows(get):
        return [get(r)[:, c * 128 : (c + 1) * 128] for r in (2, 3) for c in range(3)]

    def put_surface(ev, get):
        for h, row in enumerate(surface_rows(get)):
            ev[g, h : h + 1, :] = row

    def put_masked():
        for h, row in enumerate(surface_rows(lambda r: adj[r, 0:1, :])):
            mtab[h : h + 1, :] = row * seat[h : h + 1, :]

    half = lax.broadcasted_iota(I32, (8, 128), 1) < CAP

    def gather_adjoint():
        @pl.loop(0, NT // 8)
        def _(i):
            rows = pl.ds(pl.multiple_of(i * 8, 8), 8)
            lo, hi = slo[rows, :], shi[rows, :]
            out = jnp.zeros((8, 128), F32)
            for h in range(HI):
                table = jnp.broadcast_to(mtab[h : h + 1, :], (8, 128))
                out = jnp.where(hi == h, jnp.take_along_axis(table, lo, axis=1, mode="promise_in_bounds"), out)
            val[rows, :] = out

    def gather_forward(ev, snd):
        @pl.loop(0, NT // 8)
        def _(i):
            rows = pl.ds(pl.multiple_of(i * 8, 8), 8)
            lo, hi, owner = slo[rows, :], shi[rows, :], gi[rows, :]
            out = jnp.zeros((8, 128), F32)
            for h in range(HI):
                table = jnp.broadcast_to(ev[0, h : h + 1, :], (8, 128))
                for s in range(1, NG):
                    table = jnp.where(owner == s, ev[s, h : h + 1, :], table)
                out = jnp.where(hi == h, jnp.take_along_axis(table, lo, axis=1, mode="promise_in_bounds"), out)
            out = jnp.where(half, out, val[rows, :]) * wv[rows, :]
            snd.reshape(NT, 128)[rows, :] = out

    row_id = lax.broadcasted_iota(I32, (56, 128), 0)

    def scatter(rcv):
        def body(i, acc):
            rows = pl.ds(pl.multiple_of(i * 8, 8), 8)
            v = rcv.reshape(NT, 128)[rows, :] * rw[rows, :]
            where = rrow[rows, :]
            top = v.astype(BF16).astype(F32)
            rest = v - top
            mid = rest.astype(BF16).astype(F32)
            low = rest - mid
            blocks = []
            for j in range(8):
                hit = row_id == where[j : j + 1, :]
                blocks.append(
                    jnp.concatenate([jnp.where(hit, p[j : j + 1, :], 0.0) for p in (top, mid, low)], axis=0).astype(BF16)
                )
            m = jnp.concatenate(blocks, axis=1)
            return acc + lax.dot_general(m, onehot[i], (((1,), (1,)), ((), ())), preferred_element_type=F32)

        acc = lax.fori_loop(0, NT // 8, body, jnp.zeros((168, 128), F32))
        return acc[0:56] + acc[56:112] + acc[112:168]

    def put_forcing(total, ff):
        for h in range(HI):
            ff[2 + h // 3, 0:1, (h % 3) * 128 : (h % 3 + 1) * 128] = total[h : h + 1, :] * seat[h : h + 1, :]

    def put_terms(total, ts):
        for s in range(NG):
            ts[s, 0:HI, :] = total[8 + s * HI : 8 + (s + 1) * HI, :]

    def term_sum(tr):
        total = tr[0]
        for s in range(1, NG):
            total = total + tr[s]
        return total

    for m in range(LEV):
        mb[m] = jnp.broadcast_to(mix_ref[:, m : m + 1], (LEV, 128))
        diag = lax.broadcasted_iota(I32, (LEV, LEV), 0) == lax.broadcasted_iota(I32, (LEV, LEV), 1)
        column = jnp.sum(jnp.where(diag, mix_ref[m : m + 1, :], 0.0), axis=1, keepdims=True)
        mtb[m] = jnp.broadcast_to(column, (LEV, 128))
    for r in (0, 1):
        f1[2 + r] = strip(init_ref, r)
        sp[2 + r] = strip(spread_ref, r)
        t0[2 + r] = strip(traj_ref.at[0], r)
        t2[2 + r] = strip(traj_ref.at[2], r)
        own1[2 + r] = strip(traj_ref.at[1], r)
        own3[2 + r] = strip(traj_ref.at[3], r)
        xa[2 + r] = own3[2 + r] * strip(cot_ref, r)
    for r in (2, 3):
        u1[r] = mix_row(xa, r, mtb)
    put_surface(ev1, lambda r: f1[r, 0:1, :])

    pl.semaphore_wait(barrier, NT + NG - 2)
    gather_send(S0, ev1)
    halo_send(SP, sp)
    halo_send(U1, u1)
    halo_send(T2, t2)
    halo_send(F1, f1)
    halo_send(T0, t0)

    for h in range(HI):
        seat[h : h + 1, :] = sea_ref[h // 3 : h // 3 + 1, (h % 3) * 128 : (h % 3 + 1) * 128].astype(F32)
    diag = lax.broadcasted_iota(I32, (NT, NT), 0) == lax.broadcasted_iota(I32, (NT, NT), 1)
    live = jnp.sum(jnp.where(diag, cnt_ref[...].astype(F32), 0.0), axis=1, keepdims=True)
    slot = lax.broadcasted_iota(I32, (NT, CAP), 1).astype(F32)
    weight = w_ref[...] * jnp.where(slot < live, 1.0, 0.0)
    ones = jnp.ones((NT, CAP), F32)
    wv[...] = jnp.concatenate([weight, ones], axis=1)
    rw[...] = jnp.concatenate([ones, weight], axis=1)
    srcc, dstc, srcg = srcc_ref[...], dst_ref[...], srcg_ref[...]
    gi[...] = jnp.concatenate([srcg, srcg], axis=1)
    send_cell = jnp.concatenate([srcc, dstc], axis=1)
    slo[...] = jnp.bitwise_and(send_cell, 127)
    shi[...] = jnp.right_shift(send_cell, 7)
    rlo[...] = jnp.concatenate([jnp.bitwise_and(dstc, 127), jnp.bitwise_and(srcc, 127)], axis=1)
    rrow[...] = jnp.concatenate([jnp.right_shift(dstc, 7), 8 + HI * srcg + jnp.right_shift(srcc, 7)], axis=1)

    halo_recv(SP, sp)
    halo_recv(U1, u1)
    halo_recv(T2, t2)
    sp[0:2] = jnp.where(t > 0, sp[0:2], 0.0)
    sp[4:6] = jnp.where(t < NT - 1, sp[4:6], 0.0)
    adjoint_pair(u1, t2)
    put_masked()
    gather_adjoint()
    wait_bytes(rsem, S0, ev1.at[0 : NG - 1])
    gather_forward(ev1, snd1)
    slots_send(A1, snd1, rcv1)

    for r in (2, 3):
        xa[r] = own1[r] * adj[r]
    for r in (2, 3):
        u2[r] = mix_row(xa, r, mtb)
    halo_send(U2, u2)

    cell = lax.broadcasted_iota(I32, (128, 128), 0)

    @pl.loop(0, NT // 8)
    def _(i):
        rows = rlo[pl.ds(pl.multiple_of(i * 8, 8), 8), :]
        for j in range(8):
            hit = jnp.where(cell == rows[j : j + 1, :], 1.0, 0.0).astype(BF16)
            onehot[i, :, j * 128 : (j + 1) * 128] = hit

    halo_recv(F1, f1)
    halo_recv(T0, t0)
    halo_sent(F1, f1)
    wait_bytes(rsem, A1, rcv1.at[0 : NT - 1])
    total = scatter(rcv1)
    put_forcing(total, ff1)
    halo_send(FF1, ff1)
    put_terms(total, ts1)
    sum_send(TB1, ts1, tr1)
    halo_recv(FF1, ff1)
    for r in range(6):
        f1[r, 0:1, :] = f1[r, 0:1, :] + ff1[r]

    def put_f2(r, value):
        f2[r] = value

    forward_pair(f1, t0, lambda r: own1[r], put_f2)
    put_surface(ev2, lambda r: f2[r, 0:1, :])
    gather_send(S1, ev2)
    halo_send(F2, f2)

    wait_bytes(rsem, TB1, tr1.at[0 : NG - 1])
    part = term_sum(tr1)
    for h in range(HI):
        ls = slice((h % 3) * 128, (h % 3 + 1) * 128)
        q1[2 + h // 3, 0:1, ls] = part[h : h + 1, :] * own1[2 + h // 3, 0:1, ls]
    halo_send(Q1, q1)
    halo_recv(U2, u2)
    halo_sent(U2, u2)
    halo_recv(Q1, q1)
    for r in range(6):
        u2[r] = u2[r] + jnp.concatenate([mtb[0]] * 3, axis=1) * q1[r]
    adjoint_pair(u2, t0)
    put_masked()
    gather_adjoint()
    wait_bytes(rsem, S1, ev2.at[0 : NG - 1])
    gather_forward(ev2, snd2)
    slots_send(A2, snd2, rcv2)
    halo_recv(F2, f2)
    halo_sent(F2, f2)

    wait_bytes(ssem, S0, ev1.at[0 : NG - 1])
    wait_bytes(ssem, S1, ev2.at[0 : NG - 1])
    wait_bytes(ssem, TB1, tr1.at[0 : NG - 1])
    wait_bytes(ssem, A1, rcv1.at[0 : NT - 1])
    for k, buf in ((SP, sp), (U1, u1), (T2, t2), (T0, t0), (FF1, ff1), (Q1, q1)):
        halo_sent(k, buf)

    wait_bytes(rsem, A2, rcv2.at[0 : NT - 1])
    total = scatter(rcv2)
    put_forcing(total, ff2)
    halo_send(FF2, ff2)
    put_terms(total, ts2)
    sum_send(TB2, ts2, tr2)
    halo_recv(FF2, ff2)
    for r in range(6):
        f2[r, 0:1, :] = f2[r, 0:1, :] + ff2[r]

    def put_out(r, value):
        outf_ref[:, r - 2, :] = value

    forward_pair(f2, t2, lambda r: own3[r], put_out)
    wait_bytes(rsem, TB2, tr2.at[0 : NG - 1])
    part = term_sum(tr2)
    for h in range(HI):
        ls = slice((h % 3) * 128, (h % 3 + 1) * 128)
        adj[2 + h // 3, 0:1, ls] = adj[2 + h // 3, 0:1, ls] + part[h : h + 1, :]
    for r in (2, 3):
        outg_ref[:, r - 2, :] = adj[r]
    wait_bytes(ssem, A2, rcv2.at[0 : NT - 1])
    halo_sent(FF2, ff2)
    wait_bytes(ssem, TB2, tr2.at[0 : NG - 1])


def per_device(
    initial, cotangent, spread_coef, trajectory, mixing, sea_mask, src_group, src_cell, weight, counts, dst_cell
):
    field = lambda rows: pltpu.VMEM((rows, LEV, COLS), F32)
    line = pltpu.VMEM((6, 1, COLS), F32)
    eight = pltpu.VMEM((NG, 8, 128), F32)
    slots = pltpu.VMEM((NT, 1, 128), F32)
    columns = pltpu.VMEM((LEV, LEV, 128), F32)
    table = pltpu.VMEM((8, 128), F32)
    ints = pltpu.VMEM((NT, 128), I32)
    floats = pltpu.VMEM((NT, 128), F32)
    final, gradient = pl.pallas_call(
        kernel,
        out_shape=[jax.ShapeDtypeStruct((LEV, 2, COLS), F32)] * 2,
        in_specs=[pl.BlockSpec(memory_space=pltpu.VMEM)] * 11,
        out_specs=[pl.BlockSpec(memory_space=pltpu.VMEM)] * 2,
        scratch_shapes=[field(6)] * 7
        + [line] * 3
        + [eight] * 6
        + [slots] * 4
        + [field(6)] * 7
        + [columns] * 2
        + [table] * 2
        + [ints, ints, ints, floats, ints, ints, floats, floats]
        + [pltpu.VMEM((NT // 8, 128, 1024), BF16)]
        + [pltpu.SemaphoreType.DMA((16,))] * 2,
        compiler_params=pltpu.CompilerParams(
            collective_id=0, has_side_effects=True, vmem_limit_bytes=40 * 1024 * 1024
        ),
    )(
        initial[0], cotangent[0], spread_coef[0], trajectory[:, 0], mixing[0], sea_mask[0],
        src_group[0, 0], src_cell[0, 0], weight[0, 0], counts[0], dst_cell[0, 0],
    )
    return final[None], gradient[None]


def solution(mesh):
    return jax.shard_map(
        per_device,
        mesh=mesh,
        in_specs=(
            P("comp", None, "tile", None),
            P("comp", None, "tile", None),
            P("comp", None, "tile", None),
            P(None, "comp", None, "tile", None),
            P("comp", None, None),
            P("comp", "tile", None),
            P("comp", "tile", None, None),
            P("comp", "tile", None, None),
            P("comp", "tile", None, None),
            P("comp", "tile", None),
            P("comp", "tile", None, None),
        ),
        out_specs=(P("comp", None, "tile", None), P("comp", None, "tile", None)),
        check_vma=False,
    )
```

time: 541 us -> 76 us (0.14)
  other arithmetic: 171 us -> 0 us
  local copies, waits for them, and re-layouts: 128 us -> 3.75 us
  blocking collectives: 93.4 us -> 0 us
  starting transfers between devices: 86.2 us -> 0 us
  Pallas kernels: 0 us -> 71.2 us
  waiting for transfers between devices: 54.4 us -> 0 us
    scatter-add x8 -> x0, other arithmetic: 163 us -> none  [the longest x2 85.8 us: couple_forward(): jax.ops.segment_sum(received.reshape(-1), dst_flat, num_segments=cell_count)]
    gather x6 -> x0, local copies, waits for them, and re-layouts: 118 us -> none  [the longest x4 68.7 us: couple_forward(): values = send_weight * everyone[gather_index]]
    pallas_call x0 -> x1, Pallas kernels: none -> 71.2 us  [per_device(): pl.pallas_call(kernel, out_shape=[jax.ShapeDtypeStruct((LEV, 2, COLS), F3...]
    all_to_all x4 -> x0, starting transfers between devices: 54.5 us -> none  [slot_exchange(): lax.all_to_all(values, 'tile', split_axis=0, concat_axis=0, tiled=True)]
    unnamed x2 -> x0, blocking collectives: 52.7 us -> none
    all_to_all x4 -> x0, waiting for transfers between devices: 44.5 us -> none  [slot_exchange(): lax.all_to_all(values, 'tile', split_axis=0, concat_axis=0, tiled=True)]
    all_gather x2 -> x0, blocking collectives: 40.6 us -> none  [couple_forward(): everyone = lax.all_gather(surface, 'comp', axis=0, tiled=True).reshape(-1)]
    ppermute x16 -> x0, starting transfers between devices: 31.7 us -> none  [the longest x8 21.4 us: with_halo(): lax.ppermute(lax.slice_in_dim(block, block.shape[dim] - width, None, axis...]
  transfers between devices with their start and end apart: 20 -> 0, of which waited for: 8 -> 0; matrix products, arithmetic and copies ran while one was open for 13% -> 0% of each run, Pallas kernels for 0% -> 0%
where the time goes in v1:
time: 76 us; the launch traced here: 75.7 us
  Pallas kernels  71.2 us (94%)
  local copies, waits for them, and re-layouts  3.75 us (5%)
    pallas_call x1, Pallas kernels, per_device(): pl.pallas_call(kernel, out_shape=[jax.ShapeDtypeStruct((LEV, 2, COLS), F3...  71.2 us
    unnamed x25, local copies, waits for them, and re-layouts  3.75 us

profile of v1, /device:TPU:1, one launch (start us, length us, event | category | flops | bytes accessed | tf_op | source)
XLA Modules:
  0.0 75.7 jit_solution(7440132006292854293)
XLA Ops:
  0.6 0.0 copy-start.8
  0.6 0.0 copy-start.7
  0.7 0.7 copy.19
  1.4 0.0 copy-start.6
  1.4 0.0 copy-start
  1.4 0.9 %copy.13 = s32[1,1,96,64]{3,2,1,0:T(8,128)S(1)} copy(s32[1,1,96,64]{2,3,1,0:T(8,128)} %param.17) | data formatting | bytes 49152 | tf_op args[6]
  2.2 0.0 copy-done.6
  2.3 0.1 copy.14
  2.3 0.0 copy-done.7
  2.3 0.0 copy-start.3
  2.4 0.1 copy.15
  2.4 0.0 copy-done.8
  2.5 0.0 copy-start.1
  2.5 0.0 copy-start.2
  2.5 0.0 copy-start.4
  2.5 0.1 copy.16
  2.6 0.0 copy-start.5
  2.6 0.0 copy-done
  2.6 0.5 copy-done.3
  3.1 0.1 copy-done.1
  3.2 0.0 copy-done.2
  3.3 0.0 copy-done.4
  3.3 0.0 copy-done.5
  3.3 71.2 %shard_map.122 = (f32[12,2,384]{2,1,0:T(2,128)S(1)}, f32[12,2,384]{2,1,0:T(2,128)S(1)}) custom-call(f32[12,2,384]{2,1,0:T(2,128)S(1)} %bitcast.20, f32[12,2,384]{2,1,0:T(2,128)S(1)} %bitcast.21, f32[12,2,384]{2,1,0:T(2,128)S(1)} %bitcast.22, f32[4,12,2,384]{3,2,1,0:T(2,128)S(1)} %bitcast.19, f32[12,12]{1,0:T(8,128)S(1)} %bitcast.25, s32[2,384]{1,0:T(2,128)S(1)} %bitcast.26, ...), custom_call_target="tpu_custom_call" | custom-call | tf_op jit(solution)/shard_map/pallas_call | solution.py:368
  74.5 0.6 copy.22
  75.1 0.6 copy.23
Async XLA Ops:
  0.6 1.8 %copy-start.8 = (s32[1,1,96,64]{2,3,1,0:T(8,128)S(1)}, s32[1,1,96,64]{2,3,1,0:T(8,128)}, u32[]{:S(2)}) copy-start(s32[1,1,96,64]{2,3,1,0:T(8,128)} %param.21) | copy-start | bytes 73732
  0.6 1.7 %copy-start.7 = (f32[1,1,96,64]{2,3,1,0:T(8,128)S(1)}, f32[1,1,96,64]{2,3,1,0:T(8,128)}, u32[]{:S(2)}) copy-start(f32[1,1,96,64]{2,3,1,0:T(8,128)} %param.19) | copy-start | bytes 73732
  1.4 0.9 %copy-start.6 = (s32[1,1,96,64]{2,3,1,0:T(8,128)S(1)}, s32[1,1,96,64]{2,3,1,0:T(8,128)}, u32[]{:S(2)}) copy-start(s32[1,1,96,64]{2,3,1,0:T(8,128)} %param.18) | copy-start | bytes 73732
  1.4 1.2 %copy-start = (f32[4,1,12,2,384]{4,3,2,1,0:T(2,128)S(1)}, f32[4,1,12,2,384]{4,3,2,1,0:T(2,128)}, u32[]{:S(2)}) copy-start(f32[4,1,12,2,384]{4,3,2,1,0:T(2,128)} %param.14) | copy-start | bytes 442372
  2.3 0.8 %copy-start.3 = (f32[1,12,2,384]{3,2,1,0:T(2,128)S(1)}, f32[1,12,2,384]{3,2,1,0:T(2,128)}, u32[]{:S(2)}) copy-start(f32[1,12,2,384]{3,2,1,0:T(2,128)} %param.13) | copy-start | bytes 110596
  2.5 0.8 %copy-start.1 = (f32[1,12,2,384]{3,2,1,0:T(2,128)S(1)}, f32[1,12,2,384]{3,2,1,0:T(2,128)}, u32[]{:S(2)}) copy-start(f32[1,12,2,384]{3,2,1,0:T(2,128)} %param.11) | copy-start | bytes 110596
  2.5 0.8 %copy-start.2 = (f32[1,12,2,384]{3,2,1,0:T(2,128)S(1)}, f32[1,12,2,384]{3,2,1,0:T(2,128)}, u32[]{:S(2)}) copy-start(f32[1,12,2,384]{3,2,1,0:T(2,128)} %param.12) | copy-start | bytes 110596
  2.5 0.8 %copy-start.4 = (s32[1,2,384]{2,1,0:T(2,128)S(1)}, s32[1,2,384]{2,1,0:T(2,128)}, u32[]{:S(2)}) copy-start(s32[1,2,384]{2,1,0:T(2,128)} %param.16) | copy-start | bytes 9220
  2.6 0.7 copy-start.5

commit v2 on v1

v2 whole, which is shorter than its diff:
```python
import functools

import jax
import jax.numpy as jnp
from jax import lax
from jax.experimental import pallas as pl
from jax.experimental.pallas import tpu as pltpu
from jax.sharding import PartitionSpec as P

MESH = pl.DeviceIdType.MESH
SPREAD = 0.12
NG, NATM, NT, LEV, COLS, CAP = 8, 6, 96, 12, 384, 64
NY, NZ = 8, 12
HI = 6
BLOCKS = NT // 8
F32, BF16, I32 = jnp.float32, jnp.bfloat16, jnp.int32

S0, SP, U1, T2, F1, T0, A1, U2, TB1, F2, S1, A2, TB2, ST, DN = range(15)


def tile_offsets():
    offsets = [(a, b) for a in range(NY) for b in range(NZ) if (a, b) != (0, 0)]
    return sorted(offsets, key=lambda o: -(min(o[0], NY - o[0]) + min(o[1], NZ - o[1])))


def kernel(
    init_ref, cot_ref, spread_ref, traj_ref, mix_ref, sea_ref, srcg_ref, srcc_ref, w_ref, cnt_ref, dst_ref,
    outf_ref, outg_ref,
    sp, u1, t2, f1, t0, u2, f2, wa, xa, ya, wb, own1, own3, adj,
    st, dn, ev1, ev2, ts1, ts2, tr1, tr2, snd1, snd2, rcv1, rcv2,
    mb, mtb, seat, mtab, gi, slo, shi, rlo, rrow, rloh, rrowh, wv, rw, val, onehot, onehot_h,
    ssem, rsem,
):
    g = lax.axis_index("comp")
    t = lax.axis_index("tile")
    y, z = t // NZ, lax.rem(t, NZ)
    right, left = lax.rem(t + 1, NT), lax.rem(t + NT - 1, NT)
    atmos = g < NATM
    ocean = g >= NATM
    me = jnp.where(atmos, g, g - NATM)
    sides = (left, t, right)
    ys = [lax.rem(y + a, NY) * NZ for a in range(NY)]
    zs = [lax.rem(z + b, NZ) for b in range(NZ)]
    tiles = [ys[a] + zs[b] for a, b in tile_offsets()]

    def each_partner(act):
        @pl.when(atmos)
        def _():
            for p in range(NG - NATM):
                act(p, NATM + p)

        @pl.when(ocean)
        def _():
            for p in range(NATM):
                act(p, p)

    barrier = pltpu.get_barrier_semaphore()

    def greet(dev):
        pl.semaphore_signal(barrier, inc=1, device_id=dev, device_id_type=MESH)

    each_partner(lambda p, d: [greet((d, s)) for s in (t, left, right)])
    for dev in tiles:
        greet((g, dev))

    def remote(k, src, dst, dev):
        return pltpu.make_async_remote_copy(
            src_ref=src, dst_ref=dst, send_sem=ssem.at[k], recv_sem=rsem.at[k], device_id=dev, device_id_type=MESH
        )

    def halo_send(k, buf):
        remote(k, buf.at[2:4], buf.at[0:2], (g, right)).start()
        remote(k, buf.at[2:4], buf.at[4:6], (g, left)).start()

    def rim_send(k, buf):
        remote(k, buf.at[3:4], buf.at[1:2], (g, right)).start()
        remote(k, buf.at[2:3], buf.at[4:5], (g, left)).start()

    def wait_bytes(sem, k, ref):
        pltpu.make_async_copy(ref, ref, sem.at[k]).wait()

    def partner_wait(sem, k, buf):
        @pl.when(atmos)
        def _():
            wait_bytes(sem, k, buf.at[0 : NG - NATM])

        @pl.when(ocean)
        def _():
            wait_bytes(sem, k, buf.at[0:NATM])

    def side_wait(sem, k, buf):
        @pl.when(atmos)
        def _():
            wait_bytes(sem, k, buf.at[0, 0 : 3 * (NG - NATM)])

        @pl.when(ocean)
        def _():
            wait_bytes(sem, k, buf.at[0, 0 : 3 * NATM])

    def gather_send(k, sent, ev):
        each_partner(lambda p, d: remote(k, sent, ev.at[me], (d, t)).start())

    def slots_send(k, snd, rcv):
        for d in tiles:
            remote(k, snd.at[:, d], rcv.at[:, t], (g, d)).start()
        rcv[:, t] = snd[:, t]

    lane = lax.broadcasted_iota(I32, (LEV, COLS), 1)

    def laplace(w, r):
        mid = w[r]
        west = jnp.where(lane == 0, 0.0, pltpu.roll(mid, 1, 1))
        east = jnp.where(lane == COLS - 1, 0.0, pltpu.roll(mid, COLS - 1, 1))
        return w[r + 1] + w[r - 1] + east + west - 4.0 * mid

    def mix_row(x, r, cols):
        parts = []
        for c in range(3):
            ls = slice(c * 128, (c + 1) * 128)
            acc = cols[0] * x[r, 0:1, ls]
            for m in range(1, LEV):
                acc = acc + cols[m] * x[r, m : m + 1, ls]
            parts.append(acc)
        return jnp.concatenate(parts, axis=1)

    def forward_pair(f, ta, tb_row, put):
        for r in range(6):
            wa[r] = sp[r] * f[r]
        for r in range(1, 5):
            xa[r] = f[r] + SPREAD * sp[r] * laplace(wa, r)
        for r in range(1, 5):
            row = ta[r] * mix_row(xa, r, mb)
            ya[r] = row
            wb[r] = sp[r] * row
        for r in (2, 3):
            xa[r] = ya[r] + SPREAD * sp[r] * laplace(wb, r)
        for r in (2, 3):
            put(r, tb_row(r) * mix_row(xa, r, mb))

    def adjoint_pair(u, ta):
        for r in range(6):
            wa[r] = sp[r] * u[r]
        for r in range(1, 5):
            xa[r] = ta[r] * (u[r] + SPREAD * sp[r] * laplace(wa, r))
        for r in range(1, 5):
            row = mix_row(xa, r, mtb)
            ya[r] = row
            wb[r] = sp[r] * row
        for r in (2, 3):
            adj[r] = ya[r] + SPREAD * sp[r] * laplace(wb, r)

    def surface_rows(ref):
        return [ref[r, 0:1, c * 128 : (c + 1) * 128] for r in (2, 3) for c in range(3)]

    def put_surface(sent, ref):
        for h, row in enumerate(surface_rows(ref)):
            sent[h : h + 1, :] = row

    def put_masked():
        for h, row in enumerate(surface_rows(adj)):
            mtab[h : h + 1, :] = row * seat[h : h + 1, :]

    half = lax.broadcasted_iota(I32, (8, 128), 1) < CAP

    def pick(table, lo):
        return jnp.take_along_axis(table, lo, axis=1, mode="promise_in_bounds")

    def gather_adjoint():
        def body(i, carry):
            rows = pl.ds(pl.multiple_of(i * 8, 8), 8)
            lo, hi = slo[rows, :], shi[rows, :]
            out = jnp.zeros((8, 128), F32)
            for h in range(HI):
                table = jnp.broadcast_to(mtab[h : h + 1, :], (8, 128))
                out = jnp.where(hi == h, pick(table, lo), out)
            val[pl.ds(pl.multiple_of(i * 8 + 8, 8), 8), :] = out
            return carry

        lax.fori_loop(0, BLOCKS, body, 0, unroll=4)

    def gather_forward(ev):
        def body(i, carry):
            rows = pl.ds(pl.multiple_of(i * 8, 8), 8)
            lo, hi, owner = slo[rows, :], shi[rows, :], gi[rows, :]
            out = jnp.zeros((8, 128), F32)
            for h in range(HI):
                table = jnp.broadcast_to(ev[0, h : h + 1, :], (8, 128))
                for s in range(1, NATM):
                    table = jnp.where(owner == s, ev[s, h : h + 1, :], table)
                out = jnp.where(hi == h, pick(table, lo), out)
            here = pl.ds(pl.multiple_of(i * 8 + 8, 8), 8)
            val[here, :] = jnp.where(half, out, val[here, :]) * wv[rows, :]
            return carry

        lax.fori_loop(0, BLOCKS, body, 0, unroll=4)

    def put_slots(snd):
        own, beside = snd.at[0].reshape(NT, 128), snd.at[1].reshape(NT, 128)
        own[...] = val[8 : 8 + NT, :]
        beside[...] = jnp.where(
            lax.broadcasted_iota(I32, (NT, 128), 1) < CAP,
            val[7 : 7 + NT, :], pltpu.roll(val[9 : 9 + NT, :], CAP, 1),
        )

    def scatter(rcv, factor, index, hot, count):
        row_id = lax.broadcasted_iota(I32, (count, 128), 0)

        def body(i, acc):
            rows = pl.ds(pl.multiple_of(i * 8, 8), 8)
            v = rcv.reshape(NT, 128)[rows, :]
            if factor is not None:
                v = v * factor[rows, :]
            where = index[rows, :]
            top = v.astype(BF16).astype(F32)
            rest = v - top
            mid = rest.astype(BF16).astype(F32)
            low = rest - mid
            blocks = []
            for j in range(8):
                hit = row_id == where[j : j + 1, :]
                blocks.append(
                    jnp.concatenate([jnp.where(hit, p[j : j + 1, :], 0.0) for p in (top, mid, low)], axis=0).astype(BF16)
                )
            m = jnp.concatenate(blocks, axis=1)
            return acc + lax.dot_general(m, hot[i], (((1,), (1,)), ((), ())), preferred_element_type=F32)

        acc = lax.fori_loop(0, BLOCKS, body, jnp.zeros((3 * count, 128), F32), unroll=BLOCKS)
        return acc[0:count] + acc[count : 2 * count] + acc[2 * count : 3 * count]

    def scatter_own(rcv):
        return scatter(rcv.at[0], rw, rrow, onehot, 48)

    def scatter_beside(rcv):
        return scatter(rcv.at[1], None, rrowh, onehot_h, 16)

    def put_terms(total, ts):
        for p in range(NATM):
            ts[p, 0:HI, :] = total[8 + p * HI : 8 + (p + 1) * HI, :]

    def add_forcing(f, own, beside):
        for r in range(6):
            part = beside if r in (0, 1, 4, 5) else own
            first = {0: 0, 1: 3, 2: 0, 3: 3, 4: 8, 5: 11}[r]
            for c in range(3):
                ls = slice(c * 128, (c + 1) * 128)
                f[r, 0:1, ls] = f[r, 0:1, ls] + part[first + c : first + c + 1, :] * st[r, 1:2, ls]

    def term_sum(slots):
        total = slots[0] + slots[1]
        for p in range(2, NATM):
            total = total + jnp.where(ocean, slots[p], 0.0)
        return total

    for m in range(LEV):
        row = mix_ref[m]
        diag = lax.broadcasted_iota(I32, (LEV, LEV), 0) == lax.broadcasted_iota(I32, (LEV, LEV), 1)
        column = jnp.sum(jnp.where(diag, row, 0.0), axis=1, keepdims=True)
        mtb[m] = jnp.broadcast_to(column, (LEV, 128))
        for n in range(LEV):
            mb[n, m : m + 1, :] = jnp.broadcast_to(row[:, n : n + 1], (1, 128))
    for r in (0, 1):
        f1[2 + r] = init_ref[:, r, :]
        sp[2 + r] = spread_ref[:, r, :]
        t2[2 + r] = traj_ref[2, :, r, :]
        own3[2 + r] = traj_ref[3, :, r, :]
        xa[2 + r] = own3[2 + r] * cot_ref[:, r, :]
        st[2 + r, 0:1, :] = traj_ref[1, 0, r : r + 1, :]
        st[2 + r, 1:2, :] = sea_ref[r : r + 1, :].astype(F32)
    for r in (2, 3):
        u1[r] = mix_row(xa, r, mtb)
    put_surface(ev1.at[NATM], f1)

    pl.semaphore_wait(barrier, NT - 1 + jnp.where(atmos, 3 * (NG - NATM), 3 * NATM))
    gather_send(S0, ev1.at[NATM], ev1)
    halo_send(SP, sp)
    halo_send(U1, u1)
    rim_send(T2, t2)
    halo_send(ST, st)
    remote(DN, dst_ref, dn.at[0], (g, right)).start()
    remote(DN, dst_ref, dn.at[1], (g, left)).start()

    for r in (0, 1):
        t0[2 + r] = traj_ref[0, :, r, :]
        own1[2 + r] = traj_ref[1, :, r, :]
    for h in range(HI):
        seat[h : h + 1, :] = st[2 + h // 3, 1:2, (h % 3) * 128 : (h % 3 + 1) * 128]
    live = lax.broadcasted_iota(I32, (CAP, NT), 0) < cnt_ref[...]
    weight = jnp.where(live, w_ref[...], 0.0)
    ones = jnp.ones((CAP, NT), F32)
    wv[...] = jnp.concatenate([weight, ones], axis=0).T
    rw[...] = jnp.concatenate([ones, weight], axis=0).T
    srcc, dstc = srcc_ref[...], dst_ref[...]
    srcg = srcg_ref[...] - jnp.where(atmos, NATM, 0)
    gi[...] = jnp.concatenate([srcg, srcg], axis=0).T
    send_cell = jnp.concatenate([srcc, dstc], axis=0).T
    slo[...] = jnp.bitwise_and(send_cell, 127)
    shi[...] = jnp.right_shift(send_cell, 7)
    rlo[...] = jnp.bitwise_and(jnp.concatenate([dstc, srcc], axis=0), 127).T
    rrow[...] = jnp.concatenate([jnp.right_shift(dstc, 7), 8 + HI * srcg + jnp.right_shift(srcc, 7)], axis=0).T
    val[0:8, :] = jnp.zeros((8, 128), F32)
    val[8 + NT : 16 + NT, :] = jnp.zeros((8, 128), F32)

    wait_bytes(rsem, SP, sp.at[0:4])
    wait_bytes(rsem, U1, u1.at[0:4])
    wait_bytes(rsem, T2, t2.at[0:2])
    sp[0:2] = jnp.where(t > 0, sp[0:2], 0.0)
    sp[4:6] = jnp.where(t < NT - 1, sp[4:6], 0.0)
    halo_send(F1, f1)
    rim_send(T0, t0)
    adjoint_pair(u1, t2)
    put_masked()
    gather_adjoint()
    partner_wait(rsem, S0, ev1)
    gather_forward(ev1)
    put_slots(snd1)
    slots_send(A1, snd1, rcv1)

    for r in (2, 3):
        xa[r] = own1[r] * adj[r]
    for r in (2, 3):
        u2[r] = mix_row(xa, r, mtb)
    halo_send(U2, u2)

    wait_bytes(rsem, DN, dn)
    nearby = jnp.concatenate([dn[0], dn[1]], axis=0)
    rloh[...] = jnp.bitwise_and(nearby, 127).T
    rrowh[...] = (
        jnp.right_shift(nearby, 7) + jnp.where(lax.broadcasted_iota(I32, (2 * CAP, NT), 0) < CAP, 0, 8)
    ).T
    cell = lax.broadcasted_iota(I32, (128, 128), 0)

    @pl.loop(0, BLOCKS)
    def _(i):
        block = pl.ds(pl.multiple_of(i * 8, 8), 8)
        for index, hot in ((rlo, onehot), (rloh, onehot_h)):
            rows = index[block, :]
            for j in range(8):
                hit = jnp.where(cell == rows[j : j + 1, :], 1.0, 0.0).astype(BF16)
                hot[i, :, j * 128 : (j + 1) * 128] = hit

    wait_bytes(rsem, F1, f1.at[0:4])
    wait_bytes(rsem, T0, t0.at[0:2])
    wait_bytes(rsem, ST, st.at[0:4])
    wait_bytes(rsem, U2, u2.at[0:4])
    wait_bytes(ssem, F1, f1.at[0:4])
    wait_bytes(ssem, U2, u2.at[0:4])
    wait_bytes(rsem, A1, rcv1.at[:, 0 : NT - 1])
    own = scatter_own(rcv1)
    put_terms(own, ts1)
    each_partner(
        lambda p, d: [remote(TB1, ts1.at[p], tr1.at[2 - k, me], (d, s)).start() for k, s in enumerate(sides)]
    )
    add_forcing(f1, own, scatter_beside(rcv1))
    forward_pair(f1, t0, lambda r: own1[r], lambda r, value: f2.__setitem__(r, value))
    put_surface(ev2.at[NATM], f2)
    gather_send(S1, ev2.at[NATM], ev2)
    halo_send(F2, f2)

    side_wait(rsem, TB1, tr1.reshape(1, 3 * NATM, 8, 128))
    for k in range(3):
        part = term_sum(tr1.at[k])
        for i in range(2):
            r = 2 * k + i
            for c in range(3):
                ls = slice(c * 128, (c + 1) * 128)
                q = part[3 * i + c : 3 * i + c + 1, :] * st[r, 0:1, ls]
                u2[r, :, ls] = u2[r, :, ls] + mtb[0] * q
    adjoint_pair(u2, t0)
    put_masked()
    gather_adjoint()
    partner_wait(rsem, S1, ev2)
    gather_forward(ev2)
    put_slots(snd2)
    slots_send(A2, snd2, rcv2)

    wait_bytes(rsem, F2, f2.at[0:4])
    wait_bytes(ssem, F2, f2.at[0:4])
    partner_wait(ssem, S0, ev1)
    partner_wait(ssem, S1, ev2)
    side_wait(ssem, TB1, tr1.reshape(1, 3 * NATM, 8, 128))
    wait_bytes(ssem, A1, rcv1.at[:, 0 : NT - 1])
    wait_bytes(ssem, SP, sp.at[0:4])
    wait_bytes(ssem, U1, u1.at[0:4])
    wait_bytes(ssem, T2, t2.at[0:2])
    wait_bytes(ssem, T0, t0.at[0:2])
    wait_bytes(ssem, ST, st.at[0:4])
    wait_bytes(ssem, DN, dn)

    wait_bytes(rsem, A2, rcv2.at[:, 0 : NT - 1])
    own = scatter_own(rcv2)
    put_terms(own, ts2)
    each_partner(lambda p, d: remote(TB2, ts2.at[p], tr2.at[me], (d, t)).start())
    add_forcing(f2, own, scatter_beside(rcv2))
    forward_pair(f2, t2, lambda r: own3[r], lambda r, value: outf_ref.__setitem__((slice(None), r - 2, slice(None)), value))
    partner_wait(rsem, TB2, tr2)
    part = term_sum(tr2)
    for h in range(HI):
        ls = slice((h % 3) * 128, (h % 3 + 1) * 128)
        adj[2 + h // 3, 0:1, ls] = adj[2 + h // 3, 0:1, ls] + part[h : h + 1, :]
    for r in (2, 3):
        outg_ref[:, r - 2, :] = adj[r]
    wait_bytes(ssem, A2, rcv2.at[:, 0 : NT - 1])
    partner_wait(ssem, TB2, tr2)


def per_device(
    initial, cotangent, spread_coef, trajectory, mixing, sea_mask, src_group, src_cell, weight, counts, dst_cell
):
    vmem = lambda *shape, dtype=F32: pltpu.VMEM(shape, dtype)
    field = vmem(6, LEV, COLS)
    final, gradient = pl.pallas_call(
        kernel,
        out_shape=[jax.ShapeDtypeStruct((LEV, 2, COLS), F32)] * 2,
        in_specs=[pl.BlockSpec(memory_space=pltpu.VMEM)] * 11,
        out_specs=[pl.BlockSpec(memory_space=pltpu.VMEM)] * 2,
        scratch_shapes=[field] * 14
        + [vmem(6, 2, COLS), vmem(2, CAP, NT, dtype=I32)]
        + [vmem(NATM + 1, 8, 128)] * 2
        + [vmem(NATM, 8, 128)] * 2
        + [vmem(3, NATM, 8, 128), vmem(NATM, 8, 128)]
        + [vmem(2, NT, 1, 128)] * 4
        + [vmem(LEV, LEV, 128)] * 2
        + [vmem(8, 128)] * 2
        + [vmem(NT, 128, dtype=I32)] * 7
        + [vmem(NT, 128)] * 2
        + [vmem(NT + 16, 128)]
        + [vmem(BLOCKS, 128, 1024, dtype=BF16)] * 2
        + [pltpu.SemaphoreType.DMA((15,))] * 2,
        compiler_params=pltpu.CompilerParams(
            collective_id=0, has_side_effects=True, vmem_limit_bytes=40 * 1024 * 1024
        ),
    )(
        initial[0], cotangent[0], spread_coef[0], trajectory[:, 0], jnp.transpose(mixing, (1, 0, 2)), sea_mask[0],
        src_group[0, 0].T, src_cell[0, 0].T, weight[0, 0].T, counts[0], dst_cell[0, 0].T,
    )
    return final[None], gradient[None]


def solution(mesh):
    return jax.shard_map(
        per_device,
        mesh=mesh,
        in_specs=(
            P("comp", None, "tile", None),
            P("comp", None, "tile", None),
            P("comp", None, "tile", None),
            P(None, "comp", None, "tile", None),
            P("comp", None, None),
            P("comp", "tile", None),
            P("comp", "tile", None, None),
            P("comp", "tile", None, None),
            P("comp", "tile", None, None),
            P("comp", "tile", None),
            P("comp", "tile", None, None),
        ),
        out_specs=(P("comp", None, "tile", None), P("comp", None, "tile", None)),
        check_vma=False,
    )
```

time: 76 us -> 69.5 us (0.914)
  Pallas kernels: 71.2 us -> 60 us
  local copies, waits for them, and re-layouts: 3.75 us -> 8.16 us
    pallas_call x1, Pallas kernels: 71.2 us -> 60 us  [per_device(): pl.pallas_call(kernel, out_shape=[jax.ShapeDtypeStruct((LEV, 2, COLS), F3...]
    unnamed x25 -> x24, local copies, waits for them, and re-layouts: 3.75 us -> 8.16 us
where the time goes in v2:
time: 69.5 us; the launch traced here: 68.9 us
  Pallas kernels  60 us (86%)
  local copies, waits for them, and re-layouts  8.16 us (12%)
    pallas_call x1, Pallas kernels, per_device(): pl.pallas_call(kernel, out_shape=[jax.ShapeDtypeStruct((LEV, 2, COLS), F3...  60 us
    unnamed x24, local copies, waits for them, and re-layouts  8.16 us

profile of v2, /device:TPU:1, one launch (start us, length us, event | category | flops | bytes accessed | tf_op | source)
XLA Modules:
  0.0 68.9 jit_solution(4005331663563090154)
XLA Ops:
  0.6 0.0 copy-start.8
  0.6 0.0 copy-start.9
  0.7 0.0 copy-start.10
  0.7 0.7 copy-done.8
  1.3 0.0 copy-done.9
  1.3 0.0 copy-done.10
  1.3 0.0 copy-start
  1.3 0.9 %copy-done = f32[4,1,12,2,384]{4,3,2,1,0:T(2,128)S(1)} copy-done((f32[4,1,12,2,384]{4,3,2,1,0:T(2,128)S(1)}, f32[4,1,12,2,384]{4,3,2,1,0:T(2,128)}, u32[]{:S(2)}) %copy-start) | copy-done | bytes 147480
  2.2 0.0 copy-start.1
  2.3 0.8 %copy-done.1 = f32[1,12,2,384]{3,2,1,0:T(2,128)S(1)} copy-done((f32[1,12,2,384]{3,2,1,0:T(2,128)S(1)}, f32[1,12,2,384]{3,2,1,0:T(2,128)}, u32[]{:S(2)}) %copy-start.1) | copy-done | bytes 36888
  3.0 0.0 copy-start.2
  3.0 0.8 %copy-done.2 = f32[1,12,2,384]{3,2,1,0:T(2,128)S(1)} copy-done((f32[1,12,2,384]{3,2,1,0:T(2,128)S(1)}, f32[1,12,2,384]{3,2,1,0:T(2,128)}, u32[]{:S(2)}) %copy-start.2) | copy-done | bytes 36888
  3.8 0.0 copy-start.3
  3.8 0.8 %copy-done.3 = f32[1,12,2,384]{3,2,1,0:T(2,128)S(1)} copy-done((f32[1,12,2,384]{3,2,1,0:T(2,128)S(1)}, f32[1,12,2,384]{3,2,1,0:T(2,128)}, u32[]{:S(2)}) %copy-start.3) | copy-done | bytes 36888
  4.6 0.0 copy-start.4
  4.6 0.8 %copy-done.4 = s32[1,1,96,64]{2,3,1,0:T(8,128)S(1)} copy-done((s32[1,1,96,64]{2,3,1,0:T(8,128)S(1)}, s32[1,1,96,64]{2,3,1,0:T(8,128)}, u32[]{:S(2)}) %copy-start.4) | copy-done | bytes 24600
  5.3 0.0 copy-start.5
  5.3 0.8 %copy-done.5 = s32[1,1,96,64]{2,3,1,0:T(8,128)S(1)} copy-done((s32[1,1,96,64]{2,3,1,0:T(8,128)S(1)}, s32[1,1,96,64]{2,3,1,0:T(8,128)}, u32[]{:S(2)}) %copy-start.5) | copy-done | bytes 24600
  6.1 0.0 copy-start.6
  6.1 0.8 %copy-done.6 = f32[1,1,96,64]{2,3,1,0:T(8,128)S(1)} copy-done((f32[1,1,96,64]{2,3,1,0:T(8,128)S(1)}, f32[1,1,96,64]{2,3,1,0:T(8,128)}, u32[]{:S(2)}) %copy-start.6) | copy-done | bytes 24600
  6.8 0.0 copy-start.7
  6.8 0.8 %copy-done.7 = s32[1,1,96,64]{2,3,1,0:T(8,128)S(1)} copy-done((s32[1,1,96,64]{2,3,1,0:T(8,128)S(1)}, s32[1,1,96,64]{2,3,1,0:T(8,128)}, u32[]{:S(2)}) %copy-start.7) | copy-done | bytes 24600
  7.6 60.0 %shard_map.122 = (f32[12,2,384]{2,1,0:T(2,128)S(1)}, f32[12,2,384]{2,1,0:T(2,128)S(1)}) custom-call(f32[12,2,384]{2,1,0:T(2,128)S(1)} %bitcast.22, f32[12,2,384]{2,1,0:T(2,128)S(1)} %bitcast.23, f32[12,2,384]{2,1,0:T(2,128)S(1)} %bitcast.24, f32[4,12,2,384]{3,2,1,0:T(2,128)S(1)} %bitcast.21, f32[12,1,12]{2,1,0:T(1,128)S(1)} %bitcast.31, ...), custom_call_target="tpu_custom_call" | custom-call | tf_op jit(solution)/shard_map/pallas_call | solution.py:411
  67.6 0.6 copy.15
  68.2 0.6 copy.16
Async XLA Ops:
  0.6 0.7 %copy-start.8 = (f32[1,12,12]{2,0,1:T(1,128)S(1)}, f32[1,12,12]{2,0,1:T(1,128)}, u32[]{:S(2)}) copy-start(f32[1,12,12]{2,0,1:T(1,128)} %param.15) | copy-start | bytes 1732
  0.6 0.7 %copy-start.9 = (s32[1,2,384]{2,1,0:T(2,128)S(1)}, s32[1,2,384]{2,1,0:T(2,128)}, u32[]{:S(2)}) copy-start(s32[1,2,384]{2,1,0:T(2,128)} %param.16) | copy-start | bytes 9220
  0.7 0.7 copy-start.10
  1.3 0.9 %copy-start = (f32[4,1,12,2,384]{4,3,2,1,0:T(2,128)S(1)}, f32[4,1,12,2,384]{4,3,2,1,0:T(2,128)}, u32[]{:S(2)}) copy-start(f32[4,1,12,2,384]{4,3,2,1,0:T(2,128)} %param.14) | copy-start | bytes 442372
  2.2 0.8 %copy-start.1 = (f32[1,12,2,384]{3,2,1,0:T(2,128)S(1)}, f32[1,12,2,384]{3,2,1,0:T(2,128)}, u32[]{:S(2)}) copy-start(f32[1,12,2,384]{3,2,1,0:T(2,128)} %param.11) | copy-start | bytes 110596
  3.0 0.8 %copy-start.2 = (f32[1,12,2,384]{3,2,1,0:T(2,128)S(1)}, f32[1,12,2,384]{3,2,1,0:T(2,128)}, u32[]{:S(2)}) copy-start(f32[1,12,2,384]{3,2,1,0:T(2,128)} %param.12) | copy-start | bytes 110596
  3.8 0.8 %copy-start.3 = (f32[1,12,2,384]{3,2,1,0:T(2,128)S(1)}, f32[1,12,2,384]{3,2,1,0:T(2,128)}, u32[]{:S(2)}) copy-start(f32[1,12,2,384]{3,2,1,0:T(2,128)} %param.13) | copy-start | bytes 110596
  4.6 0.8 %copy-start.4 = (s32[1,1,96,64]{2,3,1,0:T(8,128)S(1)}, s32[1,1,96,64]{2,3,1,0:T(8,128)}, u32[]{:S(2)}) copy-start(s32[1,1,96,64]{2,3,1,0:T(8,128)} %param.17) | copy-start | bytes 73732
  5.3 0.8 %copy-start.5 = (s32[1,1,96,64]{2,3,1,0:T(8,128)S(1)}, s32[1,1,96,64]{2,3,1,0:T(8,128)}, u32[]{:S(2)}) copy-start(s32[1,1,96,64]{2,3,1,0:T(8,128)} %param.18) | copy-start | bytes 73732
  6.1 0.8 %copy-start.6 = (f32[1,1,96,64]{2,3,1,0:T(8,128)S(1)}, f32[1,1,96,64]{2,3,1,0:T(8,128)}, u32[]{:S(2)}) copy-start(f32[1,1,96,64]{2,3,1,0:T(8,128)} %param.19) | copy-start | bytes 73732
  6.8 0.8 %copy-start.7 = (s32[1,1,96,64]{2,3,1,0:T(8,128)S(1)}, s32[1,1,96,64]{2,3,1,0:T(8,128)}, u32[]{:S(2)}) copy-start(s32[1,1,96,64]{2,3,1,0:T(8,128)} %param.21) | copy-start | bytes 73732

commit v3 on v2

v3 whole, which is shorter than its diff:
```python
import functools

import jax
import jax.numpy as jnp
from jax import lax
from jax.experimental import pallas as pl
from jax.experimental.pallas import tpu as pltpu
from jax.sharding import PartitionSpec as P

MESH = pl.DeviceIdType.MESH
SPREAD = 0.12
NG, NATM, NT, LEV, COLS, CAP = 8, 6, 96, 12, 384, 64
NY, NZ = 8, 12
HI = 6
BLOCKS = NT // 8
F32, BF16, I32 = jnp.float32, jnp.bfloat16, jnp.int32

LOAD_ORDER = (4, 1, 3, 2, 0, 5, 9, 10, 7, 6, 8)
EDGE, FIRST, BACK, NEXT, DN, TS, S0, A0, TO = 0, 1, 2, 3, 4, 5, 6, 8, 10


def kernel(*refs):
    sources, out_ref, held, rest = refs[:11], refs[11], refs[12:23], refs[23:]
    init_ref, cot_ref, spread_ref, traj_ref, mix_ref, sea_ref, srcg_ref, srcc_ref, w_ref, cnt_ref, dst_ref = held
    (
        f, u, te, to, sp, wa, xa, ya, wb, adj, st,
        edge_s, edge_r, first_s, first_r, back_s, back_r, next_s, next_r, dn,
        ev, ts, tro, trs, snd, rcv,
        mat, mb, mtb, seat, mtab, gi, slo, shi, wv, val, alo, arow, aw, va, flo, frow, vf, hot_a, hot_f,
        ssem, rsem, isem,
    ) = rest
    g = lax.axis_index("comp")
    t = lax.axis_index("tile")
    y, z = t // NZ, lax.rem(t, NZ)
    right, left = lax.rem(t + 1, NT), lax.rem(t + NT - 1, NT)
    atmos = g < NATM
    ocean = g >= NATM
    me = jnp.where(atmos, g, g - NATM)

    def each_partner(act):
        @pl.when(atmos)
        def _():
            for p in range(NG - NATM):
                act(p, NATM + p)

        @pl.when(ocean)
        def _():
            for p in range(NATM):
                act(p, p)

    ys = [lax.rem(y + a, NY) * NZ for a in (4, 3, 5, 2, 6, 1, 7, 0)]

    def each_tile(act):
        @pl.loop(0, NZ - 1)
        def _(m):
            b = NZ // 2 + (1 - 2 * lax.rem(m, 2)) * ((m + 1) // 2)
            other = lax.rem(z + b, NZ)
            for row in ys:
                act(row + other)

        for row in ys[:-1]:
            act(row + z)

    barrier = pltpu.get_barrier_semaphore()

    def greet(dev):
        pl.semaphore_signal(barrier, inc=1, device_id=dev, device_id_type=MESH)

    loads = [pltpu.make_async_copy(a, b, isem.at[n]) for n, (a, b) in enumerate(zip(sources, held))]
    for n in LOAD_ORDER:
        loads[n].start()
    each_partner(lambda p, d: [greet((d, s)) for s in (t, left, right)])
    each_tile(lambda d: greet((g, d)))

    def remote(k, src, dst, dev):
        return pltpu.make_async_remote_copy(
            src_ref=src, dst_ref=dst, send_sem=ssem.at[k], recv_sem=rsem.at[k], device_id=dev, device_id_type=MESH
        )

    def beside_send(k, to_left, to_right, landing):
        remote(k, to_right, landing.at[0], (g, right)).start()
        remote(k, to_left, landing.at[1], (g, left)).start()

    def wait_bytes(sem, k, ref):
        pltpu.make_async_copy(ref, ref, sem.at[k]).wait()

    def partner_wait(sem, k, buf):
        @pl.when(atmos)
        def _():
            wait_bytes(sem, k, buf.at[0 : NG - NATM])

        @pl.when(ocean)
        def _():
            wait_bytes(sem, k, buf.at[0:NATM])

    def sides_wait(sem):
        slots = trs.reshape(1, 2 * NATM, 8, 128)

        @pl.when(atmos)
        def _():
            wait_bytes(sem, TS, slots.at[0, 0 : 2 * (NG - NATM)])

        @pl.when(ocean)
        def _():
            wait_bytes(sem, TS, slots.at[0])

    def surface_send(i):
        each_partner(lambda p, d: remote(S0 + i, ev.at[i, NATM], ev.at[i, me], (d, t)).start())

    lane = lax.broadcasted_iota(I32, (LEV, COLS), 1)

    def laplace(w, r):
        mid = w[r]
        west = jnp.where(lane == 0, 0.0, pltpu.roll(mid, 1, 1))
        east = jnp.where(lane == COLS - 1, 0.0, pltpu.roll(mid, COLS - 1, 1))
        return w[r + 1] + w[r - 1] + east + west - 4.0 * mid

    def mix_row(x, r, cols):
        parts = []
        for c in range(3):
            ls = slice(c * 128, (c + 1) * 128)
            acc = cols[0] * x[r, 0:1, ls]
            for m in range(1, LEV):
                acc = acc + cols[m] * x[r, m : m + 1, ls]
            parts.append(acc)
        return jnp.concatenate(parts, axis=1)

    def forward_pair(i):
        for r in range(6):
            wa[r] = sp[r] * f[i, r]
        for r in range(1, 5):
            xa[r] = f[i, r] + SPREAD * sp[r] * laplace(wa, r)
        for r in range(1, 5):
            row = te[i, r] * mix_row(xa, r, mb)
            ya[r] = row
            wb[r] = sp[r] * row
        for r in (2, 3):
            xa[r] = ya[r] + SPREAD * sp[r] * laplace(wb, r)
        for r in (2, 3):
            f[i + 1, r] = to[i, r] * mix_row(xa, r, mb)

    def adjoint_pair(i):
        for r in range(6):
            wa[r] = sp[r] * u[i, r]
        for r in range(1, 5):
            xa[r] = te[1 - i, r] * (u[i, r] + SPREAD * sp[r] * laplace(wa, r))
        for r in range(1, 5):
            row = mix_row(xa, r, mtb)
            ya[r] = row
            wb[r] = sp[r] * row
        for r in (2, 3):
            adj[r] = ya[r] + SPREAD * sp[r] * laplace(wb, r)

    def pack(dst, rows):
        at = 0
        for row in rows:
            dst[at : at + row.shape[0], :] = row
            at += row.shape[0]

    def surface_rows(strip):
        return [strip[r, 0:1, c * 128 : (c + 1) * 128] for r in (2, 3) for c in range(3)]

    def put_surface(i):
        for h, row in enumerate(surface_rows(f.at[i])):
            ev[i, NATM, h : h + 1, :] = row

    def put_masked():
        for h, row in enumerate(surface_rows(adj)):
            mtab[h : h + 1, :] = row * seat[h : h + 1, :]

    def first_half(rows):
        return lax.broadcasted_iota(I32, (rows, 128), 1) < CAP

    def pick(table, lo):
        return jnp.take_along_axis(table, lo, axis=1, mode="promise_in_bounds")

    def gather_adjoint():
        def body(i, carry):
            rows = pl.ds(pl.multiple_of(i * 8, 8), 8)
            lo, hi = slo[rows, :], shi[rows, :]
            out = jnp.zeros((8, 128), F32)
            for h in range(HI):
                table = jnp.broadcast_to(mtab[h : h + 1, :], (8, 128))
                out = jnp.where(hi == h, pick(table, lo), out)
            val[pl.ds(pl.multiple_of(i * 8 + 8, 8), 8), :] = out
            return carry

        lax.fori_loop(0, BLOCKS, body, 0, unroll=4)

    def gather_forward(owners):
        def body(i, carry):
            rows = pl.ds(pl.multiple_of(i * 8, 8), 8)
            lo, hi, owner = slo[rows, :], shi[rows, :], gi[rows, :]
            out = jnp.zeros((8, 128), F32)
            for h in range(HI):
                table = jnp.broadcast_to(owners[0, h : h + 1, :], (8, 128))
                for s in range(1, NATM):
                    table = jnp.where(owner == s, owners[s, h : h + 1, :], table)
                out = jnp.where(hi == h, pick(table, lo), out)
            here = pl.ds(pl.multiple_of(i * 8 + 8, 8), 8)
            val[here, :] = jnp.where(first_half(8), out, val[here, :]) * wv[rows, :]
            return carry

        lax.fori_loop(0, BLOCKS, body, 0, unroll=4)

    def send_slots(i):
        own, beside = snd.at[i, 0].reshape(NT, 128), snd.at[i, 1].reshape(NT, 128)
        own[...] = val[8 : 8 + NT, :]
        beside[...] = jnp.where(first_half(NT), val[7 : 7 + NT, :], pltpu.roll(val[9 : 9 + NT, :], CAP, 1))
        each_tile(lambda d: remote(A0 + i, snd.at[i, :, d], rcv.at[i, :, t], (g, d)).start())
        rcv[i, :, t] = snd[i, :, t]

    def packed(x):
        return jnp.where(first_half(NT // 2), x[0 : NT // 2], x[NT // 2 : NT])

    def scatter(value, index, hot, blocks, count, unroll):
        row_id = lax.broadcasted_iota(I32, (count, 128), 0)

        def body(i, acc):
            rows = pl.ds(pl.multiple_of(i * 8, 8), 8)
            v, where = value[rows, :], index[rows, :]
            top = v.astype(BF16).astype(F32)
            rest = v - top
            mid = rest.astype(BF16).astype(F32)
            low = rest - mid
            parts = []
            for j in range(8):
                hit = row_id == where[j : j + 1, :]
                parts.append(
                    jnp.concatenate([jnp.where(hit, p[j : j + 1, :], 0.0) for p in (top, mid, low)], axis=0).astype(BF16)
                )
            m = jnp.concatenate(parts, axis=1)
            return acc + lax.dot_general(m, hot[i], (((1,), (1,)), ((), ())), preferred_element_type=F32)

        acc = lax.fori_loop(0, blocks, body, jnp.zeros((3 * count, 128), F32), unroll=unroll)
        return acc[0:count] + acc[count : 2 * count] + acc[2 * count : 3 * count]

    def scatter_adjoint(i):
        got = rcv.at[i, 0].reshape(NT, 128)[...]
        va[...] = jnp.where(first_half(NT // 2), pltpu.roll(got[0 : NT // 2], CAP, 1), got[NT // 2 : NT]) * aw[...]
        total = scatter(va, arow, hot_a, BLOCKS // 2, 40, 6)
        for p in range(NATM):
            ts[i, p, 0:HI, :] = total[p * HI : (p + 1) * HI, :]

    def scatter_forward(i):
        got = rcv.at[i, 0].reshape(NT, 128)[...]
        vf[0 : NT // 2, :] = jnp.where(first_half(NT // 2), got[0 : NT // 2], pltpu.roll(got[NT // 2 : NT], CAP, 1))
        vf[NT // 2 :, :] = rcv.at[i, 1].reshape(NT, 128)[...]
        total = scatter(vf, frow, hot_f, 3 * BLOCKS // 2, 24, 6)
        for r in range(6):
            first = (8, 11, 0, 3, 16, 19)[r]
            for c in range(3):
                ls = slice(c * 128, (c + 1) * 128)
                f[i, r, 0:1, ls] = f[i, r, 0:1, ls] + total[first + c : first + c + 1, :] * st[r, 1:2, ls]

    def term_sum(slots):
        total = slots[0] + slots[1]
        for p in range(2, NATM):
            total = total + jnp.where(ocean, slots[p], 0.0)
        return total

    def put_hot(index, hot, start, stop):
        cell = lax.broadcasted_iota(I32, (128, 128), 0)

        @pl.loop(start, stop)
        def _(i):
            rows = index[pl.ds(pl.multiple_of(i * 8, 8), 8), :]
            for j in range(8):
                hit = jnp.where(cell == rows[j : j + 1, :], 1.0, 0.0).astype(BF16)
                hot[i, :, j * 128 : (j + 1) * 128] = hit

    for n in LOAD_ORDER[:6]:
        loads[n].wait()
    diag = lax.broadcasted_iota(I32, (LEV, LEV), 0) == lax.broadcasted_iota(I32, (LEV, LEV), 1)
    for m in range(LEV):
        row = mix_ref[m]
        mat[m : m + 1, :] = row
        mtb[m] = jnp.broadcast_to(jnp.sum(jnp.where(diag, row, 0.0), axis=1, keepdims=True), (LEV, 128))
    for n in range(LEV):
        mb[n] = jnp.broadcast_to(mat[:, n : n + 1], (LEV, 128))
    for r in (0, 1):
        f[0, 2 + r] = init_ref[:, r, :]
        sp[2 + r] = spread_ref[:, r, :]
        te[0, 2 + r] = traj_ref[0, :, r, :]
        te[1, 2 + r] = traj_ref[2, :, r, :]
        to[0, 2 + r] = traj_ref[1, :, r, :]
        to[1, 2 + r] = traj_ref[3, :, r, :]
        xa[2 + r] = to[1, 2 + r] * cot_ref[:, r, :]
        st[2 + r, 0:1, :] = traj_ref[1, 0, r : r + 1, :]
        st[2 + r, 1:2, :] = sea_ref[r : r + 1, :].astype(F32)
    for r in (2, 3):
        u[0, r] = mix_row(xa, r, mtb)
    put_surface(0)
    for side, near in ((0, 2), (1, 3)):
        pack(edge_s.at[side], [sp[2], sp[3], u[0, 2], u[0, 3], te[1, near], st[2], st[3]])
        pack(first_s.at[side], [f[0, 2], f[0, 3], te[0, near]])

    pl.semaphore_wait(barrier, NT - 1 + jnp.where(atmos, 3 * (NG - NATM), 3 * NATM))
    beside_send(EDGE, edge_s.at[0], edge_s.at[1], edge_r)
    surface_send(0)

    for n in LOAD_ORDER[6:]:
        loads[n].wait()
    for h in range(HI):
        seat[h : h + 1, :] = st[2 + h // 3, 1:2, (h % 3) * 128 : (h % 3 + 1) * 128]
    live = lax.broadcasted_iota(I32, (CAP, NT), 0) < cnt_ref[...]
    weight = jnp.where(live, w_ref[...], 0.0)
    wv[...] = jnp.concatenate([weight, jnp.ones((CAP, NT), F32)], axis=0).T
    aw[...] = packed(jnp.concatenate([weight, weight], axis=0).T)
    srcc, dstc = srcc_ref[...], dst_ref[...]
    srcg = srcg_ref[...] - jnp.where(atmos, NATM, 0)
    gi[...] = jnp.concatenate([srcg, srcg], axis=0).T
    send_cell = jnp.concatenate([srcc, dstc], axis=0).T
    slo[...] = jnp.bitwise_and(send_cell, 127)
    shi[...] = jnp.right_shift(send_cell, 7)
    come = packed(jnp.concatenate([srcc, srcc], axis=0).T)
    alo[...] = jnp.bitwise_and(come, 127)
    arow[...] = HI * packed(gi[...]) + jnp.right_shift(come, 7)
    come = packed(jnp.concatenate([dstc, dstc], axis=0).T)
    flo[0 : NT // 2, :] = jnp.bitwise_and(come, 127)
    frow[0 : NT // 2, :] = jnp.right_shift(come, 7)
    val[0:8, :] = jnp.zeros((8, 128), F32)
    val[8 + NT : 16 + NT, :] = jnp.zeros((8, 128), F32)

    wait_bytes(rsem, EDGE, edge_r)
    beside_send(FIRST, first_s.at[0], first_s.at[1], first_r)
    for side, rows, near, inside in ((0, (0, 1), 1, t > 0), (1, (4, 5), 4, t < NT - 1)):
        got = edge_r.at[side]
        for k, r in enumerate(rows):
            sp[r] = jnp.where(inside, got[k * LEV : (k + 1) * LEV, :], 0.0)
            u[0, r] = got[(2 + k) * LEV : (3 + k) * LEV, :]
            st[r] = got[5 * LEV + 2 * k : 5 * LEV + 2 * k + 2, :]
        te[1, near] = got[4 * LEV : 5 * LEV, :]

    def unpack_pair(buf, i, landing):
        for side, rows in ((0, (0, 1)), (1, (4, 5))):
            for k, r in enumerate(rows):
                buf[i, r] = landing[side, k * LEV : (k + 1) * LEV, :]

    @pl.loop(0, 2)
    def _(i):
        adjoint_pair(i)
        put_masked()
        gather_adjoint()
        partner_wait(rsem, S0 + i, ev.at[i])
        gather_forward(ev.at[i])
        send_slots(i)

        @pl.when(i == 0)
        def _():
            for r in (2, 3):
                xa[r] = to[0, r] * adj[r]
            for r in (2, 3):
                u[1, r] = mix_row(xa, r, mtb)
            pack(back_s, [u[1, 2], u[1, 3]])
            beside_send(DN, dst_ref, dst_ref, dn)
            beside_send(BACK, back_s, back_s, back_r)
            put_hot(alo, hot_a, 0, BLOCKS // 2)
            put_hot(flo, hot_f, 0, BLOCKS // 2)
            wait_bytes(rsem, FIRST, first_r)
            unpack_pair(f, 0, first_r)
            te[0, 1] = first_r[0, 2 * LEV : 3 * LEV, :]
            te[0, 4] = first_r[1, 2 * LEV : 3 * LEV, :]
            wait_bytes(rsem, DN, dn)
            nearby = jnp.concatenate([dn[0], dn[1]], axis=0).T
            flo[NT // 2 :, :] = jnp.bitwise_and(nearby, 127)
            frow[NT // 2 :, :] = jnp.right_shift(nearby, 7) + jnp.where(first_half(NT), 8, 16)
            put_hot(flo, hot_f, BLOCKS // 2, 3 * BLOCKS // 2)
            wait_bytes(rsem, BACK, back_r)
            unpack_pair(u, 1, back_r)

        @pl.when(i == 1)
        def _():
            beside_send(NEXT, next_s, next_s, next_r)
            for k, ref in ((EDGE, edge_s), (FIRST, first_s), (BACK, back_r), (DN, dn)):
                wait_bytes(ssem, k, ref)
            partner_wait(ssem, S0, ev.at[0])
            partner_wait(ssem, S0 + 1, ev.at[1])
            partner_wait(ssem, TO, tro.at[0])
            sides_wait(ssem)
            wait_bytes(ssem, A0, rcv.at[0, :, 0 : NT - 1])
            wait_bytes(rsem, NEXT, next_r)
            unpack_pair(f, 1, next_r)

        wait_bytes(rsem, A0 + i, rcv.at[i, :, 0 : NT - 1])
        scatter_adjoint(i)
        @pl.when(i == 0)
        def _():
            each_partner(
                lambda p, d: [
                    remote(TS, ts.at[0, p], trs.at[1, me], (d, left)).start(),
                    remote(TS, ts.at[0, p], trs.at[0, me], (d, right)).start(),
                ]
            )

        each_partner(lambda p, d: remote(TO + i, ts.at[i, p], tro.at[i, me], (d, t)).start())
        scatter_forward(i)
        forward_pair(i)

        @pl.when(i == 0)
        def _():
            put_surface(1)
            surface_send(1)
            pack(next_s, [f[1, 2], f[1, 3]])
            partner_wait(rsem, TO, tro.at[0])
            sides_wait(rsem)
            for k, slots in enumerate((trs.at[0], tro.at[0], trs.at[1])):
                part = term_sum(slots)
                for e in range(2):
                    r = 2 * k + e
                    for c in range(3):
                        ls = slice(c * 128, (c + 1) * 128)
                        q = part[3 * e + c : 3 * e + c + 1, :] * st[r, 0:1, ls]
                        u[1, r, :, ls] = u[1, r, :, ls] + mtb[0] * q

    for r in (2, 3):
        out_ref[0, :, r - 2, :] = f[2, r]
        out_ref[1, :, r - 2, :] = adj[r]
    wait_bytes(ssem, NEXT, next_r)
    wait_bytes(ssem, A0 + 1, rcv.at[1, :, 0 : NT - 1])
    partner_wait(rsem, TO + 1, tro.at[1])
    part = term_sum(tro.at[1])
    for h in range(HI):
        ls = slice((h % 3) * 128, (h % 3 + 1) * 128)
        out_ref[1, 0, h // 3 : h // 3 + 1, ls] = adj[2 + h // 3, 0:1, ls] + part[h : h + 1, :]
    partner_wait(ssem, TO + 1, tro.at[1])


def per_device(
    initial, cotangent, spread_coef, trajectory, mixing, sea_mask, src_group, src_cell, weight, counts, dst_cell
):
    vmem = lambda *shape, dtype=F32: pltpu.VMEM(shape, dtype)
    field = vmem(6, LEV, COLS)
    operands = (
        initial[0], cotangent[0], spread_coef[0], trajectory[:, 0], jnp.transpose(mixing, (1, 0, 2)), sea_mask[0],
        src_group[0, 0].T, src_cell[0, 0].T, weight[0, 0].T, counts[0], dst_cell[0, 0].T,
    )
    (both,) = pl.pallas_call(
        kernel,
        out_shape=[jax.ShapeDtypeStruct((2, LEV, 2, COLS), F32)],
        in_specs=[pl.BlockSpec(memory_space=pltpu.HBM)] * 11,
        out_specs=[pl.BlockSpec(memory_space=pltpu.VMEM)],
        scratch_shapes=[pltpu.VMEM(a.shape, a.dtype) for a in operands]
        + [vmem(3, 6, LEV, COLS), vmem(2, 6, LEV, COLS), vmem(2, 6, LEV, COLS), vmem(2, 6, LEV, COLS)]
        + [field] * 6
        + [vmem(6, 2, COLS)]
        + [vmem(2, 64, COLS)] * 2
        + [vmem(2, 40, COLS)] * 2
        + [vmem(24, COLS), vmem(2, 24, COLS)] * 2
        + [vmem(2, CAP, NT, dtype=I32)]
        + [vmem(2, NATM + 1, 8, 128)]
        + [vmem(2, NATM, 8, 128)] * 3
        + [vmem(2, 2, NT, 1, 128)] * 2
        + [vmem(LEV, LEV)]
        + [vmem(LEV, LEV, 128)] * 2
        + [vmem(8, 128)] * 2
        + [vmem(NT, 128, dtype=I32)] * 3
        + [vmem(NT, 128), vmem(NT + 16, 128)]
        + [vmem(NT // 2, 128, dtype=I32)] * 2
        + [vmem(NT // 2, 128)] * 2
        + [vmem(3 * NT // 2, 128, dtype=I32)] * 2
        + [vmem(3 * NT // 2, 128)]
        + [vmem(BLOCKS // 2, 128, 1024, dtype=BF16), vmem(3 * BLOCKS // 2, 128, 1024, dtype=BF16)]
        + [pltpu.SemaphoreType.DMA((12,))] * 2
        + [pltpu.SemaphoreType.DMA((11,))],
        compiler_params=pltpu.CompilerParams(
            collective_id=0, has_side_effects=True, vmem_limit_bytes=64 * 1024 * 1024
        ),
    )(*operands)
    return both[0:1], both[1:2]


def solution(mesh):
    return jax.shard_map(
        per_device,
        mesh=mesh,
        in_specs=(
            P("comp", None, "tile", None),
            P("comp", None, "tile", None),
            P("comp", None, "tile", None),
            P(None, "comp", None, "tile", None),
            P("comp", None, None),
            P("comp", "tile", None),
            P("comp", "tile", None, None),
            P("comp", "tile", None, None),
            P("comp", "tile", None, None),
            P("comp", "tile", None),
            P("comp", "tile", None, None),
        ),
        out_specs=(P("comp", None, "tile", None), P("comp", None, "tile", None)),
        check_vma=False,
    )
```

time: 69.5 us -> 60.5 us (0.87)
  local copies, waits for them, and re-layouts: 8.16 us -> 1.43 us
  Pallas kernels: 60 us -> 58.2 us
    unnamed x24 -> x0, local copies, waits for them, and re-layouts: 8.16 us -> none
    pallas_call x1, Pallas kernels: 60 us -> 58.2 us  [per_device(): pl.pallas_call(kernel, out_shape=[jax.ShapeDtypeStruct((2, LEV, 2, COLS),...]
    slice x0 -> x1, local copies, waits for them, and re-layouts: none -> 1.43 us  [per_device(): return (both[0:1], both[1:2])]
where the time goes in v3:
time: 60.5 us; the launch traced here: 60.3 us
  Pallas kernels  58.2 us (96%)
  local copies, waits for them, and re-layouts  1.43 us (2%)
  between operations  0.64 us (1%)
    pallas_call x1, Pallas kernels, per_device(): pl.pallas_call(kernel, out_shape=[jax.ShapeDtypeStruct((2, LEV, 2, COLS),...  58.2 us
    slice x1, local copies, waits for them, and re-layouts, per_device(): return (both[0:1], both[1:2])  1.43 us

profile of v3, /device:TPU:1, one launch (start us, length us, event | category | flops | bytes accessed | tf_op | source)
XLA Modules:
  0.0 60.3 jit_solution(12246311472987743868)
XLA Ops:
  0.6 58.2 %shard_map.122 = f32[2,12,2,384]{3,2,1,0:T(2,128)} custom-call(f32[12,2,384]{2,1,0:T(2,128)} %bitcast.20, f32[12,2,384]{2,1,0:T(2,128)} %bitcast.21, f32[12,2,384]{2,1,0:T(2,128)} %bitcast.22, f32[4,12,2,384]{3,2,1,0:T(2,128)} %bitcast.19, f32[12,1,12]{2,1,0:T(1,128)} %bitcast.27, s32[2,384]{1,0:T(2,128)} %bitcast.28, s32[64,96]{1,0:T(8,128)} %bitcast.23, ...), custom_call_target="tpu_custom_call" | custom-call | tf_op jit(solution)/shard_map/pallas_call | solution.py:438
  58.8 1.4 %fusion = (f32[1,12,2,384]{3,2,1,0:T(2,128)}, f32[1,12,2,384]{3,2,1,0:T(2,128)}) fusion(f32[2,12,2,384]{3,2,1,0:T(2,128)} %shard_map.122), kind=kLoop, calls=%fused_computation | loop fusion | bytes 147456 | tf_op jit(solution)/shard_map/slice | solution.py:470

commit v4 on v3

--- a/solution.py
+++ b/solution.py
@@ -19,6 +19,11 @@
 EDGE, FIRST, BACK, NEXT, DN, TS, S0, A0, TO = 0, 1, 2, 3, 4, 5, 6, 8, 10
 
 
+def tile_offsets():
+    offsets = [(a, b) for a in range(NY) for b in range(NZ) if (a, b) != (0, 0)]
+    return sorted(offsets, key=lambda o: -(min(o[0], NY - o[0]) + min(o[1], NZ - o[1])))
+
+
 def kernel(*refs):
     sources, out_ref, held, rest = refs[:11], refs[11], refs[12:23], refs[23:]
     init_ref, cot_ref, spread_ref, traj_ref, mix_ref, sea_ref, srcg_ref, srcc_ref, w_ref, cnt_ref, dst_ref = held
@@ -26,7 +31,7 @@
         f, u, te, to, sp, wa, xa, ya, wb, adj, st,
         edge_s, edge_r, first_s, first_r, back_s, back_r, next_s, next_r, dn,
         ev, ts, tro, trs, snd, rcv,
-        mat, mb, mtb, seat, mtab, gi, slo, shi, wv, val, alo, arow, aw, va, flo, frow, vf, hot_a, hot_f,
+        mat, mb, mtb, seat, mtab, gi, slo, shi, wv, val, alo, arow, aw, va, cells, frow, vf, hot_a, hot_f,
         ssem, rsem, isem,
     ) = rest
     g = lax.axis_index("comp")
@@ -48,18 +53,13 @@
             for p in range(NATM):
                 act(p, p)
 
-    ys = [lax.rem(y + a, NY) * NZ for a in (4, 3, 5, 2, 6, 1, 7, 0)]
+    ys = [lax.rem(y + a, NY) * NZ for a in range(NY)]
+    zs = [lax.rem(z + b, NZ) for b in range(NZ)]
+    tiles = [ys[a] + zs[b] for a, b in tile_offsets()]
 
     def each_tile(act):
-        @pl.loop(0, NZ - 1)
-        def _(m):
-            b = NZ // 2 + (1 - 2 * lax.rem(m, 2)) * ((m + 1) // 2)
-            other = lax.rem(z + b, NZ)
-            for row in ys:
-                act(row + other)
-
-        for row in ys[:-1]:
-            act(row + z)
+        for d in tiles:
+            act(d)
 
     barrier = pltpu.get_barrier_semaphore()
 
@@ -69,8 +69,8 @@
     loads = [pltpu.make_async_copy(a, b, isem.at[n]) for n, (a, b) in enumerate(zip(sources, held))]
     for n in LOAD_ORDER:
         loads[n].start()
-    each_partner(lambda p, d: [greet((d, s)) for s in (t, left, right)])
     each_tile(lambda d: greet((g, d)))
+    each_partner(lambda p, d: [greet((d, s)) for s in (left, right, t)])
 
     def remote(k, src, dst, dev):
         return pltpu.make_async_remote_copy(
@@ -213,7 +213,7 @@
     def packed(x):
         return jnp.where(first_half(NT // 2), x[0 : NT // 2], x[NT // 2 : NT])
 
-    def scatter(value, index, hot, blocks, count, unroll):
+    def scatter(value, index, hot, blocks, count, unroll, side):
         row_id = lax.broadcasted_iota(I32, (count, 128), 0)
 
         def body(i, acc):
@@ -230,7 +230,7 @@
                     jnp.concatenate([jnp.where(hit, p[j : j + 1, :], 0.0) for p in (top, mid, low)], axis=0).astype(BF16)
                 )
             m = jnp.concatenate(parts, axis=1)
-            return acc + lax.dot_general(m, hot[i], (((1,), (1,)), ((), ())), preferred_element_type=F32)
+            return acc + lax.dot_general(m, hot[i], (((1,), (side,)), ((), ())), preferred_element_type=F32)
 
         acc = lax.fori_loop(0, blocks, body, jnp.zeros((3 * count, 128), F32), unroll=unroll)
         return acc[0:count] + acc[count : 2 * count] + acc[2 * count : 3 * count]
@@ -238,7 +238,7 @@
     def scatter_adjoint(i):
         got = rcv.at[i, 0].reshape(NT, 128)[...]
         va[...] = jnp.where(first_half(NT // 2), pltpu.roll(got[0 : NT // 2], CAP, 1), got[NT // 2 : NT]) * aw[...]
-        total = scatter(va, arow, hot_a, BLOCKS // 2, 40, 6)
+        total = scatter(va, arow, hot_a, BLOCKS // 2, 40, 6, 1)
         for p in range(NATM):
             ts[i, p, 0:HI, :] = total[p * HI : (p + 1) * HI, :]
 
@@ -246,7 +246,7 @@
         got = rcv.at[i, 0].reshape(NT, 128)[...]
         vf[0 : NT // 2, :] = jnp.where(first_half(NT // 2), got[0 : NT // 2], pltpu.roll(got[NT // 2 : NT], CAP, 1))
         vf[NT // 2 :, :] = rcv.at[i, 1].reshape(NT, 128)[...]
-        total = scatter(vf, frow, hot_f, 3 * BLOCKS // 2, 24, 6)
+        total = scatter(vf, frow, hot_f, 3 * BLOCKS // 2, 24, 9, 0)
         for r in range(6):
             first = (8, 11, 0, 3, 16, 19)[r]
             for c in range(3):
@@ -268,6 +268,16 @@
             for j in range(8):
                 hit = jnp.where(cell == rows[j : j + 1, :], 1.0, 0.0).astype(BF16)
                 hot[i, :, j * 128 : (j + 1) * 128] = hit
+
+    def put_hot_columns(cells, start, count):
+        target = lax.broadcasted_iota(I32, (128, 128), 1)
+
+        @pl.loop(0, count)
+        def _(i):
+            columns = pltpu.roll(cells[...], lax.rem(128 - 8 * i, 128), 1)
+            for j in range(8):
+                hit = jnp.where(target == columns[:, j : j + 1], 1.0, 0.0).astype(BF16)
+                hot_f[start + i, j * 128 : (j + 1) * 128, :] = hit
 
     for n in LOAD_ORDER[:6]:
         loads[n].wait()
@@ -292,8 +302,9 @@
         u[0, r] = mix_row(xa, r, mtb)
     put_surface(0)
     for side, near in ((0, 2), (1, 3)):
-        pack(edge_s.at[side], [sp[2], sp[3], u[0, 2], u[0, 3], te[1, near], st[2], st[3]])
-        pack(first_s.at[side], [f[0, 2], f[0, 3], te[0, near]])
+        far = 5 - near
+        pack(edge_s.at[side], [sp[near], u[0, near], sp[far] * u[0, far], te[1, near]])
+        pack(first_s.at[side], [f[0, 2], f[0, 3], te[0, near], sp[far], st[2], st[3]])
 
     pl.semaphore_wait(barrier, NT - 1 + jnp.where(atmos, 3 * (NG - NATM), 3 * NATM))
     beside_send(EDGE, edge_s.at[0], edge_s.at[1], edge_r)
@@ -316,21 +327,26 @@
     come = packed(jnp.concatenate([srcc, srcc], axis=0).T)
     alo[...] = jnp.bitwise_and(come, 127)
     arow[...] = HI * packed(gi[...]) + jnp.right_shift(come, 7)
-    come = packed(jnp.concatenate([dstc, dstc], axis=0).T)
-    flo[0 : NT // 2, :] = jnp.bitwise_and(come, 127)
-    frow[0 : NT // 2, :] = jnp.right_shift(come, 7)
+    frow[0 : NT // 2, :] = jnp.right_shift(packed(jnp.concatenate([dstc, dstc], axis=0).T), 7)
     val[0:8, :] = jnp.zeros((8, 128), F32)
     val[8 + NT : 16 + NT, :] = jnp.zeros((8, 128), F32)
 
+    beside_send(DN, dst_ref, dst_ref, dn)
+    put_hot(alo, hot_a, 0, BLOCKS // 2)
+    cells[0:CAP, 0 : NT // 2] = jnp.bitwise_and(dstc[:, 0 : NT // 2], 127)
+    cells[CAP:, 0 : NT // 2] = jnp.bitwise_and(dstc[:, NT // 2 :], 127)
+    put_hot_columns(cells, 0, BLOCKS // 2)
+
     wait_bytes(rsem, EDGE, edge_r)
     beside_send(FIRST, first_s.at[0], first_s.at[1], first_r)
-    for side, rows, near, inside in ((0, (0, 1), 1, t > 0), (1, (4, 5), 4, t < NT - 1)):
+    beyond = ((0, 1, 0, t > 0), (1, 4, 5, t < NT - 1))
+    for side, near, far, inside in beyond:
         got = edge_r.at[side]
-        for k, r in enumerate(rows):
-            sp[r] = jnp.where(inside, got[k * LEV : (k + 1) * LEV, :], 0.0)
-            u[0, r] = got[(2 + k) * LEV : (3 + k) * LEV, :]
-            st[r] = got[5 * LEV + 2 * k : 5 * LEV + 2 * k + 2, :]
-        te[1, near] = got[4 * LEV : 5 * LEV, :]
+        sp[near] = jnp.where(inside, got[0:LEV, :], 0.0)
+        u[0, near] = got[LEV : 2 * LEV, :]
+        sp[far] = jnp.where(inside, jnp.ones((LEV, COLS), F32), 0.0)
+        u[0, far] = got[2 * LEV : 3 * LEV, :]
+        te[1, near] = got[3 * LEV : 4 * LEV, :]
 
     def unpack_pair(buf, i, landing):
         for side, rows in ((0, (0, 1)), (1, (4, 5))):
@@ -353,19 +369,20 @@
             for r in (2, 3):
                 u[1, r] = mix_row(xa, r, mtb)
             pack(back_s, [u[1, 2], u[1, 3]])
-            beside_send(DN, dst_ref, dst_ref, dn)
             beside_send(BACK, back_s, back_s, back_r)
-            put_hot(alo, hot_a, 0, BLOCKS // 2)
-            put_hot(flo, hot_f, 0, BLOCKS // 2)
+            wait_bytes(rsem, DN, dn)
+            nearby = jnp.concatenate([dn[0], dn[1]], axis=0)
+            cells[:, 0:NT] = jnp.bitwise_and(nearby, 127)
+            frow[NT // 2 :, :] = jnp.right_shift(nearby.T, 7) + jnp.where(first_half(NT), 8, 16)
+            put_hot_columns(cells, BLOCKS // 2, BLOCKS)
             wait_bytes(rsem, FIRST, first_r)
             unpack_pair(f, 0, first_r)
-            te[0, 1] = first_r[0, 2 * LEV : 3 * LEV, :]
-            te[0, 4] = first_r[1, 2 * LEV : 3 * LEV, :]
-            wait_bytes(rsem, DN, dn)
-            nearby = jnp.concatenate([dn[0], dn[1]], axis=0).T
-            flo[NT // 2 :, :] = jnp.bitwise_and(nearby, 127)
-            frow[NT // 2 :, :] = jnp.right_shift(nearby, 7) + jnp.where(first_half(NT), 8, 16)
-            put_hot(flo, hot_f, BLOCKS // 2, 3 * BLOCKS // 2)
+            for side, near, far, inside in beyond:
+                got = first_r.at[side]
+                te[0, near] = got[2 * LEV : 3 * LEV, :]
+                sp[far] = jnp.where(inside, got[3 * LEV : 4 * LEV, :], 0.0)
+                for k in range(2):
+                    st[4 * side + k] = got[4 * LEV + 2 * k : 4 * LEV + 2 * k + 2, :]
             wait_bytes(rsem, BACK, back_r)
             unpack_pair(u, 1, back_r)
 
@@ -444,8 +461,8 @@
         + [vmem(3, 6, LEV, COLS), vmem(2, 6, LEV, COLS), vmem(2, 6, LEV, COLS), vmem(2, 6, LEV, COLS)]
         + [field] * 6
         + [vmem(6, 2, COLS)]
-        + [vmem(2, 64, COLS)] * 2
-        + [vmem(2, 40, COLS)] * 2
+        + [vmem(2, 48, COLS)] * 2
+        + [vmem(2, 56, COLS)] * 2
         + [vmem(24, COLS), vmem(2, 24, COLS)] * 2
         + [vmem(2, CAP, NT, dtype=I32)]
         + [vmem(2, NATM + 1, 8, 128)]
@@ -458,15 +475,15 @@
         + [vmem(NT, 128), vmem(NT + 16, 128)]
         + [vmem(NT // 2, 128, dtype=I32)] * 2
         + [vmem(NT // 2, 128)] * 2
-        + [vmem(3 * NT // 2, 128, dtype=I32)] * 2
+        + [vmem(128, 128, dtype=I32), vmem(3 * NT // 2, 128, dtype=I32)]
         + [vmem(3 * NT // 2, 128)]
-        + [vmem(BLOCKS // 2, 128, 1024, dtype=BF16), vmem(3 * BLOCKS // 2, 128, 1024, dtype=BF16)]
+        + [vmem(BLOCKS // 2, 128, 1024, dtype=BF16), vmem(3 * BLOCKS // 2, 1024, 128, dtype=BF16)]
         + [pltpu.SemaphoreType.DMA((12,))] * 2
         + [pltpu.SemaphoreType.DMA((11,))],
         compiler_params=pltpu.CompilerParams(
-            collective_id=0, has_side_effects=True, vmem_limit_bytes=64 * 1024 * 1024
+            collective_id=0, has_side_effects=True, vmem_limit_bytes=40 * 1024 * 1024
         ),
-    )(*operands)
+    )(*[pltpu.with_memory_space_constraint(a, pltpu.HBM) for a in operands])
     return both[0:1], both[1:2]
 
 

time: 60.5 us -> 57.5 us (0.950)
  Pallas kernels: 58.2 us -> 56.1 us
  local copies, waits for them, and re-layouts: 1.43 us -> 0.65 us
    pallas_call x1, Pallas kernels: 58.2 us -> 56.1 us  [per_device(): pl.pallas_call(kernel, out_shape=[jax.ShapeDtypeStruct((2, LEV, 2, COLS),...]
    slice x1, local copies, waits for them, and re-layouts: 1.43 us -> 0.65 us  [per_device(): return (both[0:1], both[1:2])]
where the time goes in v4:
time: 57.5 us; the launch traced here: 57.4 us
  Pallas kernels  56.1 us (98%)
  local copies, waits for them, and re-layouts  0.65 us (1%)
  between operations  0.64 us (1%)
    pallas_call x1, Pallas kernels, per_device(): pl.pallas_call(kernel, out_shape=[jax.ShapeDtypeStruct((2, LEV, 2, COLS),...  56.1 us

profile of v4, /device:TPU:1, one launch (start us, length us, event | category | flops | bytes accessed | tf_op | source)
XLA Modules:
  0.0 57.4 jit_solution(6399280249268601825)
XLA Ops:
  0.6 56.1 %shard_map.122 = f32[2,12,2,384]{3,2,1,0:T(2,128)S(1)} custom-call(f32[12,2,384]{2,1,0:T(2,128)} %bitcast.20, f32[12,2,384]{2,1,0:T(2,128)} %bitcast.21, f32[12,2,384]{2,1,0:T(2,128)} %bitcast.22, f32[4,12,2,384]{3,2,1,0:T(2,128)} %bitcast.19, f32[12,1,12]{2,1,0:T(1,128)} %bitcast.27, s32[2,384]{1,0:T(2,128)} %bitcast.28, s32[64,96]{1,0:T(8,128)} %bitcast.23, ...), custom_call_target="tpu_custom_call" | custom-call | tf_op jit(solution)/shard_map/pallas_call | solution.py:455
  56.7 0.6 %fusion = (f32[1,12,2,384]{3,2,1,0:T(2,128)}, f32[1,12,2,384]{3,2,1,0:T(2,128)}) fusion(f32[2,12,2,384]{3,2,1,0:T(2,128)S(1)} %shard_map.122), kind=kLoop, calls=%fused_computation | loop fusion | bytes 147456 | tf_op jit(solution)/shard_map/slice | solution.py:487

commit v5 on v4

--- a/solution.py
+++ b/solution.py
@@ -13,6 +13,8 @@
 NY, NZ = 8, 12
 HI = 6
 BLOCKS = NT // 8
+RING_Y = (4, 3, 5, 2, 6, 1, 7)
+RING_Z = (6, 5, 7, 4, 8, 3, 9, 2, 10, 1, 11)
 F32, BF16, I32 = jnp.float32, jnp.bfloat16, jnp.int32
 
 LOAD_ORDER = (4, 1, 3, 2, 0, 5, 9, 10, 7, 6, 8)
@@ -31,8 +33,8 @@
         f, u, te, to, sp, wa, xa, ya, wb, adj, st,
         edge_s, edge_r, first_s, first_r, back_s, back_r, next_s, next_r, dn,
         ev, ts, tro, trs, snd, rcv,
-        mat, mb, mtb, seat, mtab, gi, slo, shi, wv, val, alo, arow, aw, va, cells, frow, vf, hot_a, hot_f,
-        ssem, rsem, isem,
+        mat, mb, mtb, seat, mtab, gi, slo, shi, wv, val, plo, phi, pulled, alo, arow, aw, va, cells, frow, vf, hot_a, hot_f,
+        ssem, rsem, isem, known,
     ) = rest
     g = lax.axis_index("comp")
     t = lax.axis_index("tile")
@@ -69,8 +71,21 @@
     loads = [pltpu.make_async_copy(a, b, isem.at[n]) for n, (a, b) in enumerate(zip(sources, held))]
     for n in LOAD_ORDER:
         loads[n].start()
-    each_tile(lambda d: greet((g, d)))
+    for b in RING_Z:
+        greet((g, ys[0] + zs[b]))
+    column = [ys[a] + zs[0] for a in RING_Y]
+    for d in column:
+        greet((g, d))
     each_partner(lambda p, d: [greet((d, s)) for s in (left, right, t)])
+
+    @pl.when(z == 0)
+    def _():
+        greet((g, left))
+
+    @pl.when(z == NZ - 1)
+    def _():
+        greet((g, right))
+
 
     def remote(k, src, dst, dev):
         return pltpu.make_async_remote_copy(
@@ -177,15 +192,15 @@
     def gather_adjoint():
         def body(i, carry):
             rows = pl.ds(pl.multiple_of(i * 8, 8), 8)
-            lo, hi = slo[rows, :], shi[rows, :]
+            lo, hi = plo[rows, :], phi[rows, :]
             out = jnp.zeros((8, 128), F32)
             for h in range(HI):
                 table = jnp.broadcast_to(mtab[h : h + 1, :], (8, 128))
                 out = jnp.where(hi == h, pick(table, lo), out)
-            val[pl.ds(pl.multiple_of(i * 8 + 8, 8), 8), :] = out
+            pulled[rows, :] = out
             return carry
 
-        lax.fori_loop(0, BLOCKS, body, 0, unroll=4)
+        lax.fori_loop(0, BLOCKS // 2, body, 0, unroll=6)
 
     def gather_forward(owners):
         def body(i, carry):
@@ -197,16 +212,19 @@
                 for s in range(1, NATM):
                     table = jnp.where(owner == s, owners[s, h : h + 1, :], table)
                 out = jnp.where(hi == h, pick(table, lo), out)
-            here = pl.ds(pl.multiple_of(i * 8 + 8, 8), 8)
-            val[here, :] = jnp.where(first_half(8), out, val[here, :]) * wv[rows, :]
+            val[pl.ds(pl.multiple_of(i * 8 + 8, 8), 8), :] = out * wv[rows, :]
             return carry
 
         lax.fori_loop(0, BLOCKS, body, 0, unroll=4)
 
+    def put_beside(i):
+        beside = snd.at[i, 1].reshape(NT, 128)
+        beside[...] = jnp.where(first_half(NT), val[7 : 7 + NT, :], pltpu.roll(val[9 : 9 + NT, :], CAP, 1))
+
     def send_slots(i):
-        own, beside = snd.at[i, 0].reshape(NT, 128), snd.at[i, 1].reshape(NT, 128)
-        own[...] = val[8 : 8 + NT, :]
-        beside[...] = jnp.where(first_half(NT), val[7 : 7 + NT, :], pltpu.roll(val[9 : 9 + NT, :], CAP, 1))
+        own, mid = snd.at[i, 0].reshape(NT, 128), NT // 2
+        own[0:mid] = jnp.where(first_half(mid), val[8 : 8 + mid, :], pltpu.roll(pulled[...], CAP, 1))
+        own[mid:NT] = jnp.where(first_half(mid), val[8 + mid : 8 + NT, :], pulled[...])
         each_tile(lambda d: remote(A0 + i, snd.at[i, :, d], rcv.at[i, :, t], (g, d)).start())
         rcv[i, :, t] = snd[i, :, t]
 
@@ -269,12 +287,12 @@
                 hit = jnp.where(cell == rows[j : j + 1, :], 1.0, 0.0).astype(BF16)
                 hot[i, :, j * 128 : (j + 1) * 128] = hit
 
-    def put_hot_columns(cells, start, count):
+    def put_hot_columns(cells, first, start, count):
         target = lax.broadcasted_iota(I32, (128, 128), 1)
 
         @pl.loop(0, count)
         def _(i):
-            columns = pltpu.roll(cells[...], lax.rem(128 - 8 * i, 128), 1)
+            columns = pltpu.roll(cells[...], lax.rem(128 - 8 * (first + i), 128), 1)
             for j in range(8):
                 hit = jnp.where(target == columns[:, j : j + 1], 1.0, 0.0).astype(BF16)
                 hot_f[start + i, j * 128 : (j + 1) * 128, :] = hit
@@ -306,8 +324,11 @@
         pack(edge_s.at[side], [sp[near], u[0, near], sp[far] * u[0, far], te[1, near]])
         pack(first_s.at[side], [f[0, 2], f[0, 3], te[0, near], sp[far], st[2], st[3]])
 
-    pl.semaphore_wait(barrier, NT - 1 + jnp.where(atmos, 3 * (NG - NATM), 3 * NATM))
+    edge = jnp.where((z == 0) | (z == NZ - 1), 1, 0)
+    pl.semaphore_wait(barrier, NY + NZ - 2 + edge + jnp.where(atmos, 3 * (NG - NATM), 3 * NATM))
     beside_send(EDGE, edge_s.at[0], edge_s.at[1], edge_r)
+    for d in column:
+        pl.semaphore_signal(known, inc=1, device_id=(g, d), device_id_type=MESH)
     surface_send(0)
 
     for n in LOAD_ORDER[6:]:
@@ -316,29 +337,33 @@
         seat[h : h + 1, :] = st[2 + h // 3, 1:2, (h % 3) * 128 : (h % 3 + 1) * 128]
     live = lax.broadcasted_iota(I32, (CAP, NT), 0) < cnt_ref[...]
     weight = jnp.where(live, w_ref[...], 0.0)
-    wv[...] = jnp.concatenate([weight, jnp.ones((CAP, NT), F32)], axis=0).T
-    aw[...] = packed(jnp.concatenate([weight, weight], axis=0).T)
+    wv[...] = jnp.concatenate([weight, weight], axis=0).T
+    aw[...] = packed(wv[...])
     srcc, dstc = srcc_ref[...], dst_ref[...]
     srcg = srcg_ref[...] - jnp.where(atmos, NATM, 0)
     gi[...] = jnp.concatenate([srcg, srcg], axis=0).T
-    send_cell = jnp.concatenate([srcc, dstc], axis=0).T
+    send_cell = jnp.concatenate([srcc, srcc], axis=0).T
     slo[...] = jnp.bitwise_and(send_cell, 127)
     shi[...] = jnp.right_shift(send_cell, 7)
-    come = packed(jnp.concatenate([srcc, srcc], axis=0).T)
-    alo[...] = jnp.bitwise_and(come, 127)
-    arow[...] = HI * packed(gi[...]) + jnp.right_shift(come, 7)
-    frow[0 : NT // 2, :] = jnp.right_shift(packed(jnp.concatenate([dstc, dstc], axis=0).T), 7)
+    alo[...] = packed(slo[...])
+    arow[...] = HI * packed(gi[...]) + packed(shi[...])
+    come = packed(jnp.concatenate([dstc, dstc], axis=0).T)
+    plo[...] = jnp.bitwise_and(come, 127)
+    phi[...] = jnp.right_shift(come, 7)
+    frow[0 : NT // 2, :] = phi[...]
     val[0:8, :] = jnp.zeros((8, 128), F32)
     val[8 + NT : 16 + NT, :] = jnp.zeros((8, 128), F32)
 
-    beside_send(DN, dst_ref, dst_ref, dn)
     put_hot(alo, hot_a, 0, BLOCKS // 2)
     cells[0:CAP, 0 : NT // 2] = jnp.bitwise_and(dstc[:, 0 : NT // 2], 127)
     cells[CAP:, 0 : NT // 2] = jnp.bitwise_and(dstc[:, NT // 2 :], 127)
-    put_hot_columns(cells, 0, BLOCKS // 2)
-
+    put_hot_columns(cells, 0, 0, BLOCKS // 2)
+    beside_send(DN, dst_ref, dst_ref, dn)
+
+    partner_wait(rsem, S0, ev.at[0])
+    gather_forward(ev.at[0])
+    put_beside(0)
     wait_bytes(rsem, EDGE, edge_r)
-    beside_send(FIRST, first_s.at[0], first_s.at[1], first_r)
     beyond = ((0, 1, 0, t > 0), (1, 4, 5, t < NT - 1))
     for side, near, far, inside in beyond:
         got = edge_r.at[side]
@@ -353,13 +378,18 @@
             for k, r in enumerate(rows):
                 buf[i, r] = landing[side, k * LEV : (k + 1) * LEV, :]
 
+    pl.semaphore_wait(known, NY - 1)
     @pl.loop(0, 2)
     def _(i):
         adjoint_pair(i)
         put_masked()
         gather_adjoint()
-        partner_wait(rsem, S0 + i, ev.at[i])
-        gather_forward(ev.at[i])
+        @pl.when(i == 1)
+        def _():
+            partner_wait(rsem, S0 + 1, ev.at[1])
+            gather_forward(ev.at[1])
+            put_beside(1)
+
         send_slots(i)
 
         @pl.when(i == 0)
@@ -369,12 +399,40 @@
             for r in (2, 3):
                 u[1, r] = mix_row(xa, r, mtb)
             pack(back_s, [u[1, 2], u[1, 3]])
-            beside_send(BACK, back_s, back_s, back_r)
             wait_bytes(rsem, DN, dn)
             nearby = jnp.concatenate([dn[0], dn[1]], axis=0)
             cells[:, 0:NT] = jnp.bitwise_and(nearby, 127)
             frow[NT // 2 :, :] = jnp.right_shift(nearby.T, 7) + jnp.where(first_half(NT), 8, 16)
-            put_hot_columns(cells, BLOCKS // 2, BLOCKS)
+            put_hot_columns(cells, 0, BLOCKS // 2, BLOCKS // 2)
+            beside_send(FIRST, first_s.at[0], first_s.at[1], first_r)
+            beside_send(BACK, back_s, back_s, back_r)
+            put_hot_columns(cells, BLOCKS // 2, BLOCKS, BLOCKS // 2)
+
+        @pl.when(i == 1)
+        def _():
+            beside_send(NEXT, next_s, next_s, next_r)
+            for k, ref in ((EDGE, edge_s), (FIRST, first_s), (BACK, back_r), (DN, dn)):
+                wait_bytes(ssem, k, ref)
+            partner_wait(ssem, S0, ev.at[0])
+            partner_wait(ssem, S0 + 1, ev.at[1])
+            partner_wait(ssem, TO, tro.at[0])
+            sides_wait(ssem)
+            wait_bytes(ssem, A0, rcv.at[0, :, 0 : NT - 1])
+
+        wait_bytes(rsem, A0 + i, rcv.at[i, :, 0 : NT - 1])
+        scatter_adjoint(i)
+        @pl.when(i == 0)
+        def _():
+            each_partner(
+                lambda p, d: [
+                    remote(TS, ts.at[0, p], trs.at[1, me], (d, left)).start(),
+                    remote(TS, ts.at[0, p], trs.at[0, me], (d, right)).start(),
+                ]
+            )
+
+        each_partner(lambda p, d: remote(TO + i, ts.at[i, p], tro.at[i, me], (d, t)).start())
+        @pl.when(i == 0)
+        def _():
             wait_bytes(rsem, FIRST, first_r)
             unpack_pair(f, 0, first_r)
             for side, near, far, inside in beyond:
@@ -383,34 +441,12 @@
                 sp[far] = jnp.where(inside, got[3 * LEV : 4 * LEV, :], 0.0)
                 for k in range(2):
                     st[4 * side + k] = got[4 * LEV + 2 * k : 4 * LEV + 2 * k + 2, :]
-            wait_bytes(rsem, BACK, back_r)
-            unpack_pair(u, 1, back_r)
 
         @pl.when(i == 1)
         def _():
-            beside_send(NEXT, next_s, next_s, next_r)
-            for k, ref in ((EDGE, edge_s), (FIRST, first_s), (BACK, back_r), (DN, dn)):
-                wait_bytes(ssem, k, ref)
-            partner_wait(ssem, S0, ev.at[0])
-            partner_wait(ssem, S0 + 1, ev.at[1])
-            partner_wait(ssem, TO, tro.at[0])
-            sides_wait(ssem)
-            wait_bytes(ssem, A0, rcv.at[0, :, 0 : NT - 1])
             wait_bytes(rsem, NEXT, next_r)
             unpack_pair(f, 1, next_r)
 
-        wait_bytes(rsem, A0 + i, rcv.at[i, :, 0 : NT - 1])
-        scatter_adjoint(i)
-        @pl.when(i == 0)
-        def _():
-            each_partner(
-                lambda p, d: [
-                    remote(TS, ts.at[0, p], trs.at[1, me], (d, left)).start(),
-                    remote(TS, ts.at[0, p], trs.at[0, me], (d, right)).start(),
-                ]
-            )
-
-        each_partner(lambda p, d: remote(TO + i, ts.at[i, p], tro.at[i, me], (d, t)).start())
         scatter_forward(i)
         forward_pair(i)
 
@@ -419,6 +455,8 @@
             put_surface(1)
             surface_send(1)
             pack(next_s, [f[1, 2], f[1, 3]])
+            wait_bytes(rsem, BACK, back_r)
+            unpack_pair(u, 1, back_r)
             partner_wait(rsem, TO, tro.at[0])
             sides_wait(rsem)
             for k, slots in enumerate((trs.at[0], tro.at[0], trs.at[1])):
@@ -474,12 +512,14 @@
         + [vmem(NT, 128, dtype=I32)] * 3
         + [vmem(NT, 128), vmem(NT + 16, 128)]
         + [vmem(NT // 2, 128, dtype=I32)] * 2
+        + [vmem(NT // 2, 128)]
+        + [vmem(NT // 2, 128, dtype=I32)] * 2
         + [vmem(NT // 2, 128)] * 2
         + [vmem(128, 128, dtype=I32), vmem(3 * NT // 2, 128, dtype=I32)]
         + [vmem(3 * NT // 2, 128)]
         + [vmem(BLOCKS // 2, 128, 1024, dtype=BF16), vmem(3 * BLOCKS // 2, 1024, 128, dtype=BF16)]
         + [pltpu.SemaphoreType.DMA((12,))] * 2
-        + [pltpu.SemaphoreType.DMA((11,))],
+        + [pltpu.SemaphoreType.DMA((11,)), pltpu.SemaphoreType.REGULAR],
         compiler_params=pltpu.CompilerParams(
             collective_id=0, has_side_effects=True, vmem_limit_bytes=40 * 1024 * 1024
         ),

time: 57.5 us -> 53.3 us (0.927)
  Pallas kernels: 56.1 us -> 51.9 us
    pallas_call x1, Pallas kernels: 56.1 us -> 51.9 us  [per_device(): pl.pallas_call(kernel, out_shape=[jax.ShapeDtypeStruct((2, LEV, 2, COLS),...]
where the time goes in v5:
time: 53.3 us; the launch traced here: 53.1 us
  Pallas kernels  51.9 us (97%)
  local copies, waits for them, and re-layouts  0.65 us (1%)
  between operations  0.64 us (1%)
    pallas_call x1, Pallas kernels, per_device(): pl.pallas_call(kernel, out_shape=[jax.ShapeDtypeStruct((2, LEV, 2, COLS),...  51.9 us

profile of v5, /device:TPU:1, one launch (start us, length us, event | category | flops | bytes accessed | tf_op | source)
XLA Modules:
  0.0 53.1 jit_solution(1811380499346190151)
XLA Ops:
  0.6 51.9 %shard_map.122 = f32[2,12,2,384]{3,2,1,0:T(2,128)S(1)} custom-call(f32[12,2,384]{2,1,0:T(2,128)} %bitcast.20, f32[12,2,384]{2,1,0:T(2,128)} %bitcast.21, f32[12,2,384]{2,1,0:T(2,128)} %bitcast.22, f32[4,12,2,384]{3,2,1,0:T(2,128)} %bitcast.19, f32[12,1,12]{2,1,0:T(1,128)} %bitcast.27, s32[2,384]{1,0:T(2,128)} %bitcast.28, s32[64,96]{1,0:T(8,128)} %bitcast.23, ...), custom_call_target="tpu_custom_call" | custom-call | tf_op jit(solution)/shard_map/pallas_call | solution.py:493
  52.5 0.6 %fusion = (f32[1,12,2,384]{3,2,1,0:T(2,128)}, f32[1,12,2,384]{3,2,1,0:T(2,128)}) fusion(f32[2,12,2,384]{3,2,1,0:T(2,128)S(1)} %shard_map.122), kind=kLoop, calls=%fused_computation | loop fusion | bytes 147456 | tf_op jit(solution)/shard_map/slice | solution.py:527

commit v6 on v5

--- a/solution.py
+++ b/solution.py
@@ -14,7 +14,7 @@
 HI = 6
 BLOCKS = NT // 8
 RING_Y = (4, 3, 5, 2, 6, 1, 7)
-RING_Z = (6, 5, 7, 4, 8, 3, 9, 2, 10, 1, 11)
+NEAR_Z = (4, 8, 3, 9, 2, 10, 1, 11)
 F32, BF16, I32 = jnp.float32, jnp.bfloat16, jnp.int32
 
 LOAD_ORDER = (4, 1, 3, 2, 0, 5, 9, 10, 7, 6, 8)
@@ -34,7 +34,7 @@
         edge_s, edge_r, first_s, first_r, back_s, back_r, next_s, next_r, dn,
         ev, ts, tro, trs, snd, rcv,
         mat, mb, mtb, seat, mtab, gi, slo, shi, wv, val, plo, phi, pulled, alo, arow, aw, va, cells, frow, vf, hot_a, hot_f,
-        ssem, rsem, isem, known,
+        ssem, rsem, isem, known, known_row,
     ) = rest
     g = lax.axis_index("comp")
     t = lax.axis_index("tile")
@@ -71,7 +71,7 @@
     loads = [pltpu.make_async_copy(a, b, isem.at[n]) for n, (a, b) in enumerate(zip(sources, held))]
     for n in LOAD_ORDER:
         loads[n].start()
-    for b in RING_Z:
+    for b in NEAR_Z:
         greet((g, ys[0] + zs[b]))
     column = [ys[a] + zs[0] for a in RING_Y]
     for d in column:
@@ -215,7 +215,7 @@
             val[pl.ds(pl.multiple_of(i * 8 + 8, 8), 8), :] = out * wv[rows, :]
             return carry
 
-        lax.fori_loop(0, BLOCKS, body, 0, unroll=4)
+        lax.fori_loop(0, BLOCKS, body, 0, unroll=6)
 
     def put_beside(i):
         beside = snd.at[i, 1].reshape(NT, 128)
@@ -325,7 +325,7 @@
         pack(first_s.at[side], [f[0, 2], f[0, 3], te[0, near], sp[far], st[2], st[3]])
 
     edge = jnp.where((z == 0) | (z == NZ - 1), 1, 0)
-    pl.semaphore_wait(barrier, NY + NZ - 2 + edge + jnp.where(atmos, 3 * (NG - NATM), 3 * NATM))
+    pl.semaphore_wait(barrier, NY - 1 + len(NEAR_Z) + edge + jnp.where(atmos, 3 * (NG - NATM), 3 * NATM))
     beside_send(EDGE, edge_s.at[0], edge_s.at[1], edge_r)
     for d in column:
         pl.semaphore_signal(known, inc=1, device_id=(g, d), device_id_type=MESH)
@@ -360,6 +360,9 @@
     put_hot_columns(cells, 0, 0, BLOCKS // 2)
     beside_send(DN, dst_ref, dst_ref, dn)
 
+    pl.semaphore_wait(known, NY - 1)
+    for b in (2, NZ - 2):
+        pl.semaphore_signal(known_row, inc=1, device_id=(g, ys[0] + zs[b]), device_id_type=MESH)
     partner_wait(rsem, S0, ev.at[0])
     gather_forward(ev.at[0])
     put_beside(0)
@@ -378,7 +381,6 @@
             for k, r in enumerate(rows):
                 buf[i, r] = landing[side, k * LEV : (k + 1) * LEV, :]
 
-    pl.semaphore_wait(known, NY - 1)
     @pl.loop(0, 2)
     def _(i):
         adjoint_pair(i)
@@ -389,6 +391,10 @@
             partner_wait(rsem, S0 + 1, ev.at[1])
             gather_forward(ev.at[1])
             put_beside(1)
+
+        @pl.when(i == 0)
+        def _():
+            pl.semaphore_wait(known_row, 2)
 
         send_slots(i)
 
@@ -519,7 +525,7 @@
         + [vmem(3 * NT // 2, 128)]
         + [vmem(BLOCKS // 2, 128, 1024, dtype=BF16), vmem(3 * BLOCKS // 2, 1024, 128, dtype=BF16)]
         + [pltpu.SemaphoreType.DMA((12,))] * 2
-        + [pltpu.SemaphoreType.DMA((11,)), pltpu.SemaphoreType.REGULAR],
+        + [pltpu.SemaphoreType.DMA((11,)), pltpu.SemaphoreType.REGULAR, pltpu.SemaphoreType.REGULAR],
         compiler_params=pltpu.CompilerParams(
             collective_id=0, has_side_effects=True, vmem_limit_bytes=40 * 1024 * 1024
         ),

time: 53.3 us -> 53.2 us (level)
  no operation moved by 1% of the time
where the time goes in v6:
time: 53.2 us; the launch traced here: 53 us
  Pallas kernels  51.7 us (97%)
  local copies, waits for them, and re-layouts  0.65 us (1%)
  between operations  0.64 us (1%)
    pallas_call x1, Pallas kernels, per_device(): pl.pallas_call(kernel, out_shape=[jax.ShapeDtypeStruct((2, LEV, 2, COLS),...  51.7 us

profile of v6, /device:TPU:1, one launch (start us, length us, event | category | flops | bytes accessed | tf_op | source)
XLA Modules:
  0.0 53.0 jit_solution(9100998036530997030)
XLA Ops:
  0.6 51.7 %shard_map.122 = f32[2,12,2,384]{3,2,1,0:T(2,128)S(1)} custom-call(f32[12,2,384]{2,1,0:T(2,128)} %bitcast.20, f32[12,2,384]{2,1,0:T(2,128)} %bitcast.21, f32[12,2,384]{2,1,0:T(2,128)} %bitcast.22, f32[4,12,2,384]{3,2,1,0:T(2,128)} %bitcast.19, f32[12,1,12]{2,1,0:T(1,128)} %bitcast.27, s32[2,384]{1,0:T(2,128)} %bitcast.28, s32[64,96]{1,0:T(8,128)} %bitcast.23, ...), custom_call_target="tpu_custom_call" | custom-call | tf_op jit(solution)/shard_map/pallas_call | solution.py:499
  52.4 0.6 %fusion = (f32[1,12,2,384]{3,2,1,0:T(2,128)}, f32[1,12,2,384]{3,2,1,0:T(2,128)}) fusion(f32[2,12,2,384]{3,2,1,0:T(2,128)S(1)} %shard_map.122), kind=kLoop, calls=%fused_computation | loop fusion | bytes 147456 | tf_op jit(solution)/shard_map/slice | solution.py:533

commit v7 on v6

--- a/solution.py
+++ b/solution.py
@@ -18,7 +18,7 @@
 F32, BF16, I32 = jnp.float32, jnp.bfloat16, jnp.int32
 
 LOAD_ORDER = (4, 1, 3, 2, 0, 5, 9, 10, 7, 6, 8)
-EDGE, FIRST, BACK, NEXT, DN, TS, S0, A0, TO = 0, 1, 2, 3, 4, 5, 6, 8, 10
+EDGE, FIRST, BACK, NEXT, DN, TS, S0, A0, TO, REST = 0, 1, 2, 3, 4, 5, 6, 8, 10, 12
 
 
 def tile_offsets():
@@ -31,7 +31,7 @@
     init_ref, cot_ref, spread_ref, traj_ref, mix_ref, sea_ref, srcg_ref, srcc_ref, w_ref, cnt_ref, dst_ref = held
     (
         f, u, te, to, sp, wa, xa, ya, wb, adj, st,
-        edge_s, edge_r, first_s, first_r, back_s, back_r, next_s, next_r, dn,
+        edge_s, edge_r, rest_s, rest_r, first_s, first_r, back_s, back_r, next_s, next_r, dn,
         ev, ts, tro, trs, snd, rcv,
         mat, mb, mtb, seat, mtab, gi, slo, shi, wv, val, plo, phi, pulled, alo, arow, aw, va, cells, frow, vf, hot_a, hot_f,
         ssem, rsem, isem, known, known_row,
@@ -122,13 +122,19 @@
     def surface_send(i):
         each_partner(lambda p, d: remote(S0 + i, ev.at[i, NATM], ev.at[i, me], (d, t)).start())
 
-    lane = lax.broadcasted_iota(I32, (LEV, COLS), 1)
+    def sideways(mid):
+        column = lax.broadcasted_iota(I32, mid.shape, 1)
+        west = jnp.where(column == 0, 0.0, pltpu.roll(mid, 1, 1))
+        east = jnp.where(column == COLS - 1, 0.0, pltpu.roll(mid, COLS - 1, 1))
+        return east + west
 
     def laplace(w, r):
         mid = w[r]
-        west = jnp.where(lane == 0, 0.0, pltpu.roll(mid, 1, 1))
-        east = jnp.where(lane == COLS - 1, 0.0, pltpu.roll(mid, COLS - 1, 1))
-        return w[r + 1] + w[r - 1] + east + west - 4.0 * mid
+        return w[r + 1] + w[r - 1] + sideways(mid) - 4.0 * mid
+
+    def level_zero(x):
+        weights = jnp.concatenate([mb[0]] * 3, axis=1)
+        return jnp.sum(weights * x, axis=0, keepdims=True)
 
     def mix_row(x, r, cols):
         parts = []
@@ -159,12 +165,31 @@
             wa[r] = sp[r] * u[i, r]
         for r in range(1, 5):
             xa[r] = te[1 - i, r] * (u[i, r] + SPREAD * sp[r] * laplace(wa, r))
+        second_step()
+
+    def second_step():
         for r in range(1, 5):
             row = mix_row(xa, r, mtb)
             ya[r] = row
             wb[r] = sp[r] * row
         for r in (2, 3):
             adj[r] = ya[r] + SPREAD * sp[r] * laplace(wb, r)
+
+    def first_surface():
+        for r in (2, 3):
+            xa[r] = te[1, r] * (u[0, r] + SPREAD * sp[r] * laplace(wa, r))
+        tops = {r: level_zero(xa[r]) for r in (2, 3)}
+        coef = {r: sp[r, 0:1, :] for r in (2, 3)}
+        for side, near, far, inside in beyond:
+            inner = 2 + side
+            got = edge_r.at[side]
+            xa[near] = got[LEV : 2 * LEV, :] * wa[inner]
+            tops[near] = got[2 * LEV : 2 * LEV + 1, :] + level_zero(xa[near])
+            coef[near] = jnp.where(inside, got[2 * LEV + 1 : 2 * LEV + 2, :], 0.0)
+        scaled = {r: coef[r] * tops[r] for r in range(1, 5)}
+        for r in (2, 3):
+            around = scaled[r + 1] + scaled[r - 1] + sideways(scaled[r]) - 4.0 * scaled[r]
+            adj[r, 0:1, :] = tops[r] + SPREAD * coef[r] * around
 
     def pack(dst, rows):
         at = 0
@@ -319,9 +344,15 @@
     for r in (2, 3):
         u[0, r] = mix_row(xa, r, mtb)
     put_surface(0)
+    for r in (2, 3):
+        wa[r] = sp[r] * u[0, r]
     for side, near in ((0, 2), (1, 3)):
         far = 5 - near
-        pack(edge_s.at[side], [sp[near], u[0, near], sp[far] * u[0, far], te[1, near]])
+        product = wa[near]
+        reach = SPREAD * te[1, near] * sp[near]
+        share = te[1, near] * u[0, near] + reach * (wa[far] + sideways(product) - 4.0 * product)
+        pack(edge_s.at[side], [product, reach, level_zero(share), sp[near, 0:1, :]])
+        pack(rest_s.at[side], [share, sp[near]])
         pack(first_s.at[side], [f[0, 2], f[0, 3], te[0, near], sp[far], st[2], st[3]])
 
     edge = jnp.where((z == 0) | (z == NZ - 1), 1, 0)
@@ -358,6 +389,7 @@
     cells[0:CAP, 0 : NT // 2] = jnp.bitwise_and(dstc[:, 0 : NT // 2], 127)
     cells[CAP:, 0 : NT // 2] = jnp.bitwise_and(dstc[:, NT // 2 :], 127)
     put_hot_columns(cells, 0, 0, BLOCKS // 2)
+    beside_send(REST, rest_s.at[0], rest_s.at[1], rest_r)
     beside_send(DN, dst_ref, dst_ref, dn)
 
     pl.semaphore_wait(known, NY - 1)
@@ -369,12 +401,8 @@
     wait_bytes(rsem, EDGE, edge_r)
     beyond = ((0, 1, 0, t > 0), (1, 4, 5, t < NT - 1))
     for side, near, far, inside in beyond:
-        got = edge_r.at[side]
-        sp[near] = jnp.where(inside, got[0:LEV, :], 0.0)
-        u[0, near] = got[LEV : 2 * LEV, :]
-        sp[far] = jnp.where(inside, jnp.ones((LEV, COLS), F32), 0.0)
-        u[0, far] = got[2 * LEV : 3 * LEV, :]
-        te[1, near] = got[3 * LEV : 4 * LEV, :]
+        wa[near] = jnp.where(inside, edge_r[side, 0:LEV, :], 0.0)
+    first_surface()
 
     def unpack_pair(buf, i, landing):
         for side, rows in ((0, (0, 1)), (1, (4, 5))):
@@ -383,7 +411,10 @@
 
     @pl.loop(0, 2)
     def _(i):
-        adjoint_pair(i)
+        @pl.when(i == 1)
+        def _():
+            adjoint_pair(1)
+
         put_masked()
         gather_adjoint()
         @pl.when(i == 1)
@@ -400,24 +431,30 @@
 
         @pl.when(i == 0)
         def _():
-            for r in (2, 3):
-                xa[r] = to[0, r] * adj[r]
-            for r in (2, 3):
-                u[1, r] = mix_row(xa, r, mtb)
-            pack(back_s, [u[1, 2], u[1, 3]])
+            beside_send(FIRST, first_s.at[0], first_s.at[1], first_r)
             wait_bytes(rsem, DN, dn)
             nearby = jnp.concatenate([dn[0], dn[1]], axis=0)
             cells[:, 0:NT] = jnp.bitwise_and(nearby, 127)
             frow[NT // 2 :, :] = jnp.right_shift(nearby.T, 7) + jnp.where(first_half(NT), 8, 16)
             put_hot_columns(cells, 0, BLOCKS // 2, BLOCKS // 2)
-            beside_send(FIRST, first_s.at[0], first_s.at[1], first_r)
-            beside_send(BACK, back_s, back_s, back_r)
+            wait_bytes(rsem, REST, rest_r)
+            for side, near, far, inside in beyond:
+                xa[near] = xa[near] + rest_r[side, 0:LEV, :]
+                sp[near] = jnp.where(inside, rest_r[side, LEV : 2 * LEV, :], 0.0)
+            second_step()
+            for r in (2, 3):
+                xa[r] = to[0, r] * adj[r]
+            for r in (2, 3):
+                u[1, r] = mix_row(xa, r, mtb)
+            for side, near in ((0, 2), (1, 3)):
+                pack(back_s.at[side], [u[1, 2], u[1, 3], te[1, near]])
+            beside_send(BACK, back_s.at[0], back_s.at[1], back_r)
             put_hot_columns(cells, BLOCKS // 2, BLOCKS, BLOCKS // 2)
 
         @pl.when(i == 1)
         def _():
             beside_send(NEXT, next_s, next_s, next_r)
-            for k, ref in ((EDGE, edge_s), (FIRST, first_s), (BACK, back_r), (DN, dn)):
+            for k, ref in ((REST, rest_s), (EDGE, edge_s), (FIRST, first_s), (BACK, back_s), (DN, dn)):
                 wait_bytes(ssem, k, ref)
             partner_wait(ssem, S0, ev.at[0])
             partner_wait(ssem, S0 + 1, ev.at[1])
@@ -463,6 +500,8 @@
             pack(next_s, [f[1, 2], f[1, 3]])
             wait_bytes(rsem, BACK, back_r)
             unpack_pair(u, 1, back_r)
+            for side, near, far, inside in beyond:
+                te[1, near] = back_r[side, 2 * LEV : 3 * LEV, :]
             partner_wait(rsem, TO, tro.at[0])
             sides_wait(rsem)
             for k, slots in enumerate((trs.at[0], tro.at[0], trs.at[1])):
@@ -505,9 +544,11 @@
         + [vmem(3, 6, LEV, COLS), vmem(2, 6, LEV, COLS), vmem(2, 6, LEV, COLS), vmem(2, 6, LEV, COLS)]
         + [field] * 6
         + [vmem(6, 2, COLS)]
-        + [vmem(2, 48, COLS)] * 2
+        + [vmem(2, 2 * LEV + 2, COLS)] * 2
+        + [vmem(2, 2 * LEV, COLS)] * 2
         + [vmem(2, 56, COLS)] * 2
-        + [vmem(24, COLS), vmem(2, 24, COLS)] * 2
+        + [vmem(2, 40, COLS)] * 2
+        + [vmem(24, COLS), vmem(2, 24, COLS)]
         + [vmem(2, CAP, NT, dtype=I32)]
         + [vmem(2, NATM + 1, 8, 128)]
         + [vmem(2, NATM, 8, 128)] * 3
@@ -524,7 +565,7 @@
         + [vmem(128, 128, dtype=I32), vmem(3 * NT // 2, 128, dtype=I32)]
         + [vmem(3 * NT // 2, 128)]
         + [vmem(BLOCKS // 2, 128, 1024, dtype=BF16), vmem(3 * BLOCKS // 2, 1024, 128, dtype=BF16)]
-        + [pltpu.SemaphoreType.DMA((12,))] * 2
+        + [pltpu.SemaphoreType.DMA((13,))] * 2
         + [pltpu.SemaphoreType.DMA((11,)), pltpu.SemaphoreType.REGULAR, pltpu.SemaphoreType.REGULAR],
         compiler_params=pltpu.CompilerParams(
             collective_id=0, has_side_effects=True, vmem_limit_bytes=40 * 1024 * 1024

time: 53.2 us -> 53.2 us (level)
  no operation moved by 1% of the time
where the time goes in v7:
time: 53.2 us; the launch traced here: 53 us
  Pallas kernels  51.8 us (97%)
  local copies, waits for them, and re-layouts  0.65 us (1%)
  between operations  0.64 us (1%)
    pallas_call x1, Pallas kernels, per_device(): pl.pallas_call(kernel, out_shape=[jax.ShapeDtypeStruct((2, LEV, 2, COLS),...  51.8 us

profile of v7, /device:TPU:1, one launch (start us, length us, event | category | flops | bytes accessed | tf_op | source)
XLA Modules:
  0.0 53.0 jit_solution(15735217940033748985)
XLA Ops:
  0.6 51.8 %shard_map.122 = f32[2,12,2,384]{3,2,1,0:T(2,128)S(1)} custom-call(f32[12,2,384]{2,1,0:T(2,128)} %bitcast.20, f32[12,2,384]{2,1,0:T(2,128)} %bitcast.21, f32[12,2,384]{2,1,0:T(2,128)} %bitcast.22, f32[4,12,2,384]{3,2,1,0:T(2,128)} %bitcast.19, f32[12,1,12]{2,1,0:T(1,128)} %bitcast.27, s32[2,384]{1,0:T(2,128)} %bitcast.28, s32[64,96]{1,0:T(8,128)} %bitcast.23, ...), custom_call_target="tpu_custom_call" | custom-call | tf_op jit(solution)/shard_map/pallas_call | solution.py:538
  52.4 0.6 %fusion = (f32[1,12,2,384]{3,2,1,0:T(2,128)}, f32[1,12,2,384]{3,2,1,0:T(2,128)}) fusion(f32[2,12,2,384]{3,2,1,0:T(2,128)S(1)} %shard_map.122), kind=kLoop, calls=%fused_computation | loop fusion | bytes 147456 | tf_op jit(solution)/shard_map/slice | solution.py:574
